TPU v7x, 32 devices: a whole 2x2x4 slice. The times are simulated.
32 devices in a mesh: tm: 4 (over x, core), height: 2 (over y), width: 4 (over z).
Axes of the slice: x: 2, y: 2, z: 4, core: 2. Of those that a mesh axis runs over, the one named last changes fastest.
Arguments:
- frames: bfloat16 [8, 8, 128, 384], P('tm', 'height', 'width'), may hold values from -6 to 6
- cache_in: bfloat16 [2, 8, 128, 384], P(None, 'height', 'width'), may hold values from -6 to 6
- kernel: bfloat16 [384, 3, 3, 3, 384], replicated, may hold values from -0.0625 to 0.0625
- conv_bias: float32 [384], replicated, may hold values from -3 to 3
- cotangent: bfloat16 [8, 8, 128, 384], P('tm', 'height', 'width'), may hold values from -6 to 6
Outputs:
- decoded: bfloat16 [8, 8, 128, 384], P('tm', 'height', 'width')
- frame_grad: bfloat16 [8, 8, 128, 384], P('tm', 'height', 'width')
- cache_grad: bfloat16 [8, 8, 128, 384], P('tm', 'height', 'width')
- kernel_grad: float32 [384, 3, 3, 3, 384], P('height')
All inputs are finite; a program needn't handle non-finite values.
Results may differ from a plain program's by a relative error of at most 0.0053.
Values may be sent and summed in bfloat16 or wider, within the bound.
A program may use at most 256 MiB of HBM per device.

v0:
```python
import jax
import jax.numpy as jnp
from jax import lax
from jax.sharding import PartitionSpec as P


def shifted(value, axis, by):
    length = lax.axis_size(axis)
    pairs = [(i, i + by) for i in range(length) if 0 <= i + by < length]
    return lax.ppermute(value, axis, pairs)


def with_halo(value, sides, width):
    for axis, dim in sides:
        size, length = (lax.axis_size(axis), value.shape[dim])
        up = [(i, (i + 1) % size) for i in range(size - 1)]
        down = [(j, i) for i, j in up]
        last = lax.slice_in_dim(value, length - width, length, axis=dim)
        initial = lax.slice_in_dim(value, 0, width, axis=dim)
        before = lax.ppermute(last, axis, up)
        after = lax.ppermute(initial, axis, down)
        value = jnp.concatenate([before, value, after], axis=dim)
    return value


def tap_block(padded, tap_t, tap_h, tap_w, depth_count, row_count, col_count):
    block = padded[
        tap_t : tap_t + depth_count, tap_h : tap_h + row_count, tap_w : tap_w + col_count
    ]
    return block.reshape(-1, block.shape[-1])


def body(frames, cache_in, kernel, conv_bias, cotangent):
    frame_count, row_count, col_count, channels = frames.shape
    is_first = lax.axis_index("tm") == 0
    earlier = shifted(frames, "tm", 1)
    earlier = jnp.where(is_first, cache_in, earlier)
    stacked = jnp.concatenate([earlier, frames], 0)
    extended = with_halo(stacked, (("height", 1), ("width", 2)), 1)
    pre_act = jnp.zeros((frame_count * row_count * col_count, channels), jnp.float32) + conv_bias
    for tap_t in range(3):
        for tap_h in range(3):
            for tap_w in range(3):
                block = tap_block(extended, tap_t, tap_h, tap_w, frame_count, row_count, col_count)
                pre_act = pre_act + lax.dot_general(
                    block,
                    kernel[:, tap_t, tap_h, tap_w, :],
                    (((1,), (1,)), ((), ())),
                    preferred_element_type=jnp.float32,
                )
    sigma = jax.nn.sigmoid(pre_act)
    decoded = (pre_act * sigma).astype(jnp.bfloat16).reshape(frames.shape)
    scaled = (
        cotangent.reshape(-1, channels).astype(jnp.float32)
        * sigma
        * (1.0 + pre_act * (1.0 - sigma))
    ).astype(jnp.bfloat16)
    grad_rimmed = with_halo(scaled.reshape(frames.shape), (("height", 1), ("width", 2)), 1)
    partial_value = jnp.zeros((frame_count + 2, row_count, col_count, channels), jnp.float32)
    for tap_t in range(3):
        contrib = jnp.zeros((frame_count * row_count * col_count, channels), jnp.float32)
        for tap_h in range(3):
            for tap_w in range(3):
                block = grad_rimmed[
                    :, 2 - tap_h : 2 - tap_h + row_count, 2 - tap_w : 2 - tap_w + col_count
                ].reshape(-1, channels)
                contrib = contrib + jnp.dot(
                    block, kernel[:, tap_t, tap_h, tap_w, :], preferred_element_type=jnp.float32
                )
        partial_value = partial_value.at[tap_t : tap_t + frame_count].add(
            contrib.reshape(frame_count, row_count, col_count, channels)
        )
    cache_grad = partial_value[:2].astype(jnp.bfloat16)
    carried = shifted(cache_grad, "tm", -1)
    frame_grad = (
        partial_value[2:]
        .at[frame_count - 2 :]
        .add(carried.astype(jnp.float32))
        .astype(jnp.bfloat16)
    )
    pieces = []
    for tap_t in range(3):
        for tap_h in range(3):
            for tap_w in range(3):
                block = tap_block(extended, tap_t, tap_h, tap_w, frame_count, row_count, col_count)
                pieces.append(
                    lax.dot_general(
                        scaled, block, (((0,), (0,)), ((), ())), preferred_element_type=jnp.float32
                    )
                )
    owned = lax.psum_scatter(
        jnp.stack(pieces, 1).reshape(
            channels // lax.axis_size("height") * lax.axis_size("height"), 3, 3, 3, channels
        ),
        "height",
        scatter_dimension=0,
        tiled=True,
    )
    kernel_grad = lax.psum(owned, ("tm", "width"))
    return (decoded, frame_grad, cache_grad, kernel_grad)


def solution(mesh):
    in_specs = (
        P("tm", "height", "width", None),
        P(None, "height", "width", None),
        P(),
        P(),
        P("tm", "height", "width", None),
    )
    out_specs = (
        P("tm", "height", "width", None),
        P("tm", "height", "width", None),
        P("tm", "height", "width", None),
        P("height", None, None, None, None),
    )
    return jax.shard_map(body, mesh=mesh, in_specs=in_specs, out_specs=out_specs, check_vma=False)
```

profile of v0, /device:TPU:15, one launch (start us, length us, event | category | flops | bytes accessed | tf_op | source)
XLA Modules:
  0.0 437.5 jit_solution(14931912472405542979)
XLA Ops:
  7.2 1.3 collective-permute-start
  8.5 2.4 collective-permute-done
  11.8 1.3 collective-permute-start.1
  13.1 4.0 collective-permute-start.2
  19.6 3.2 collective-permute-start.3
  22.9 2.1 collective-permute-start.4
  24.9 1.1 pad_maximum_fusion.1
  26.3 1.3 collective-permute-done.4
  27.6 1.4 maximum_maximum_fusion
  39.4 1.1 fusion.25
  41.6 1.1 fusion.23
  46.1 1.1 fusion.19
  47.2 1.1 fusion.18
  48.3 1.1 fusion.17
  49.4 1.1 fusion.16
  51.7 1.1 fusion.14
  52.8 1.2 fusion.13
  54.0 1.2 fusion.12
  57.3 1.1 fusion.9
  58.5 1.1 fusion.8
  59.6 1.1 fusion.7
  60.7 1.1 fusion.6
  61.8 1.2 fusion.5
  63.0 1.1 fusion.4
  64.1 1.1 fusion.3
  65.2 1.1 fusion.2
  66.3 1.1 fusion.1
  67.5 1.1 fusion
  68.7 1.3 collective-permute-start.5
  70.0 4.0 collective-permute-start.6
  74.0 1.1 collective-permute-done.6
  75.2 2.1 collective-permute-start.7
  77.3 3.4 collective-permute-start.8
  80.7 1.2 fusion.70
  82.0 1.3 fusion.91
  83.3 1.2 fusion.50
  84.9 1.2 fusion.75
  86.1 1.2 convolution_add_fusion.20
  87.4 1.2 convolution_add_fusion.19
  88.6 1.2 convolution_add_fusion.18
  89.8 1.2 convolution_add_fusion.17
  91.1 1.2 convolution_add_fusion.16
  92.3 1.2 convolution_add_fusion.15
  93.6 1.2 fusion.28
  94.9 1.2 convolution_add_fusion.13
  96.1 1.2 convolution_add_fusion.12
  97.4 157.5 %reduce-scatter.2.cloned.1.call-done = f32[192,3,3,3,384]{4,0,3,2,1:T(8,128)} async-done(((f32[384,3,3,3,384]{4,0,3,2,1:T(8,128)}), f32[192,3,3,3,384]{4,0,3,2,1:T(8,128)}) %reduce-scatter.2.cloned.1.call-update) | async-done | bytes 7962640 | tf_op jit(solution)/shard_map/reduce_scatter | solution.py:91
  254.9 1.2 fusion.55
  256.2 1.2 convolution_add_fusion.11
  257.4 1.2 convolution_add_fusion.10
  258.6 1.2 convolution_add_fusion.9
  259.9 1.2 convolution_add_fusion.8
  261.1 1.2 fusion.29
  262.5 2.6 collective-permute-start.9
  265.1 1.3 fusion.35
  266.4 1.3 convolution_add_fusion.6
  267.6 1.2 convolution_add_fusion.5
  268.9 1.2 convolution_add_fusion.4
  270.1 1.2 convolution_add_fusion.3
  271.4 1.2 convolution_add_fusion.2
  272.6 1.2 convolution_add_fusion.1
  273.8 1.3 fusion.30
  275.9 147.4 %all-reduce.3.cloned.1.call-done = f32[192,3,3,3,384]{4,0,3,2,1:T(8,128)} async-done(((f32[192,3,3,3,384]{4,0,3,2,1:T(8,128)}), f32[192,3,3,3,384]{4,0,3,2,1:T(8,128)}) %all-reduce.3.cloned.1.call-update) | async-done | bytes 7962640 | tf_op jit(solution)/shard_map/psum | solution.py:99
  423.3 7.4 %copy.37 = f32[192,3,3,3,384]{4,0,3,2,1:T(8,128)} copy(f32[192,3,3,3,384]{4,0,3,2,1:T(8,128)} %all-reduce.3.cloned.1.call-done) | data formatting | bytes 15925248
  (75 shorter events, 22.9 us)
Async XLA Ops:
  7.2 247.7 %reduce-scatter.2.cloned.1.call-start = ((), (), s32[]{:S(2)}) async-start(), calls=%async_computation.1 | async-start | bytes 23887872 | tf_op jit(solution)/shard_map/reduce_scatter | solution.py:91
  7.2 3.7 collective-permute-start
  8.5 20.9 %slice-start = ((s8[7962624]{0:T(1024)(128)(4,1)}), s8[4194304]{0:T(1024)(128)(4,1)S(1)}, s32[]{:S(2)}) async-start(s8[7962624]{0:T(1024)(128)(4,1)} %bitcast.401), calls=%async_computation.3 | async-start | bytes 8388608
  11.0 18.8 %copy-start.2 = (f32[384]{0:T(512)S(1)}, f32[384]{0:T(512)}, u32[]{:S(2)}) copy-start(f32[384]{0:T(512)} %param.18) | copy-start | bytes 4612
  11.8 6.2 %collective-permute-start.1 = (bf16[4,1,32,384]{3,2,1,0:T(8,128)(2,1)S(1)}, bf16[4,1,32,384]{3,2,1,0:T(8,128)(2,1)S(1)}, u32[]{:S(2)}, u32[]{:S(2)}) collective-permute-start(bf16[4,1,32,384]{3,2,1,0:T(8,128)(2,1)S(1)} %get-tuple-element.92), channel_id=1, source_target_pairs={{0,4},{1,5},{2,6},{3,7},{8,12},{9,13},{10,14},{11,15},{16,20},{17,... | collective-permute-start | bytes 294920 | tf_op jit(solution)/shard_map/ppermute | solution.py:20
  13.1 5.6 %collective-permute-start.2 = (bf16[4,1,32,384]{3,2,1,0:T(8,128)(2,1)S(1)}, bf16[4,1,32,384]{3,2,1,0:T(8,128)(2,1)S(1)}, u32[]{:S(2)}, u32[]{:S(2)}) collective-permute-start(bf16[4,1,32,384]{3,2,1,0:T(8,128)(2,1)S(1)} %get-tuple-element.93), channel_id=1, source_target_pairs={{4,0},{5,1},{6,2},{7,3},{12,8},{13,9},{14,10},{15,11},{20,16},{21,... | collective-permute-start | bytes 294920 | tf_op jit(solution)/shard_map/ppermute | solution.py:21
  19.6 6.6 %collective-permute-start.3 = (bf16[4,6,1,384]{3,2,1,0:T(2,128)(2,1)S(1)}, bf16[4,6,1,384]{3,2,1,0:T(2,128)(2,1)S(1)}, u32[]{:S(2)}, u32[]{:S(2)}) collective-permute-start(bf16[4,6,1,384]{3,2,1,0:T(2,128)(2,1)S(1)} %get-tuple-element.80), channel_id=1, source_target_pairs={{0,1},{1,2},{2,3},{4,5},{5,6},{6,7},{8,9},{9,10},{10,11},{12,13},{... | collective-permute-start | bytes 55304 | tf_op jit(solution)/shard_map/ppermute | solution.py:20
  22.9 4.7 %collective-permute-start.4 = (bf16[4,6,1,384]{3,2,1,0:T(2,128)(2,1)S(1)}, bf16[4,6,1,384]{3,2,1,0:T(2,128)(2,1)S(1)}, u32[]{:S(2)}, u32[]{:S(2)}) collective-permute-start(bf16[4,6,1,384]{3,2,1,0:T(2,128)(2,1)S(1)} %get-tuple-element.81), channel_id=1, source_target_pairs={{1,0},{2,1},{3,2},{5,4},{6,5},{7,6},{9,8},{10,9},{11,10},{13,12},{... | collective-permute-start | bytes 55304 | tf_op jit(solution)/shard_map/ppermute | solution.py:21
  26.2 3.2 slice-start.1
  32.4 3.6 copy-start
  33.6 3.6 copy-start.3
  68.6 354.6 %all-reduce.3.cloned.1.call-start = ((), (), s32[]{:S(2)}) async-start(), calls=%async_computation.2 | async-start | bytes 15925248 | tf_op jit(solution)/shard_map/psum | solution.py:99
  68.7 5.3 %collective-permute-start.5 = (bf16[2,1,32,384]{3,2,1,0:T(8,128)(2,1)S(1)}, bf16[2,1,32,384]{3,2,1,0:T(8,128)(2,1)S(1)}, u32[]{:S(2)}, u32[]{:S(2)}) collective-permute-start(bf16[2,1,32,384]{3,2,1,0:T(8,128)(2,1)S(1)} %get-tuple-element.106), channel_id=1, source_target_pairs={{0,4},{1,5},{2,6},{3,7},{8,12},{9,13},{10,14},{11,15},{16,20},{17,... | collective-permute-start | bytes 147464 | tf_op jit(solution)/shard_map/ppermute | solution.py:20
  70.0 5.2 %collective-permute-start.6 = (bf16[2,1,32,384]{3,2,1,0:T(8,128)(2,1)S(1)}, bf16[2,1,32,384]{3,2,1,0:T(8,128)(2,1)S(1)}, u32[]{:S(2)}, u32[]{:S(2)}) collective-permute-start(bf16[2,1,32,384]{3,2,1,0:T(8,128)(2,1)S(1)} %get-tuple-element.107), channel_id=1, source_target_pairs={{4,0},{5,1},{6,2},{7,3},{12,8},{13,9},{14,10},{15,11},{20,16},{21,... | collective-permute-start | bytes 147464 | tf_op jit(solution)/shard_map/ppermute | solution.py:21
  75.2 9.3 %collective-permute-start.7 = (bf16[2,6,1,384]{3,2,1,0:T(2,128)(2,1)S(1)}, bf16[2,6,1,384]{3,2,1,0:T(2,128)(2,1)S(1)}, u32[]{:S(2)}, u32[]{:S(2)}) collective-permute-start(bf16[2,6,1,384]{3,2,1,0:T(2,128)(2,1)S(1)} %get-tuple-element.102), channel_id=1, source_target_pairs={{1,0},{2,1},{3,2},{5,4},{6,5},{7,6},{9,8},{10,9},{11,10},{13,12},{... | collective-permute-start | bytes 27656 | tf_op jit(solution)/shard_map/ppermute | solution.py:21
  77.3 7.2 %collective-permute-start.8 = (bf16[2,6,1,384]{3,2,1,0:T(2,128)(2,1)S(1)}, bf16[2,6,1,384]{3,2,1,0:T(2,128)(2,1)S(1)}, u32[]{:S(2)}, u32[]{:S(2)}) collective-permute-start(bf16[2,6,1,384]{3,2,1,0:T(2,128)(2,1)S(1)} %get-tuple-element.103), channel_id=1, source_target_pairs={{0,1},{1,2},{2,3},{4,5},{5,6},{6,7},{8,9},{9,10},{10,11},{12,13},{... | collective-permute-start | bytes 27656 | tf_op jit(solution)/shard_map/ppermute | solution.py:20
  262.5 168.1 %copy-start.1 = (bf16[2,4,32,384]{3,2,1,0:T(8,128)(2,1)}, bf16[2,4,32,384]{3,2,1,0:T(8,128)(2,1)S(1)}, u32[]{:S(2)}) copy-start(bf16[2,4,32,384]{3,2,1,0:T(8,128)(2,1)S(1)} %slice.745) | copy-start | bytes 589828
  262.5 12.6 %collective-permute-start.9 = (bf16[2,4,32,384]{3,2,1,0:T(8,128)(2,1)S(1)}, bf16[2,4,32,384]{3,2,1,0:T(8,128)(2,1)S(1)}, u32[]{:S(2)}, u32[]{:S(2)}) collective-permute-start(bf16[2,4,32,384]{3,2,1,0:T(8,128)(2,1)S(1)} %slice.745), channel_id=1, source_target_pairs={{8,0},{16,8},{24,16},{9,1},{17,9},{25,17},{10,2},{18,10},{26,18},{... | collective-permute-start | bytes 589832 | tf_op jit(solution)/shard_map/ppermute | solution.py:10
Sparse Core Ops, SparseCore 0:
  68.8 186.0 reduce-scatter.1
  259.0 164.1 all-reduce.2
where the time goes:
time: 441 us; the launch traced here: 437 us
  waiting for transfers between devices  311 us (71%)
  matrix products  72.3 us (16%)
  starting transfers between devices  25.3 us (6%)
  between operations  14.8 us (3%)
  local copies, waits for them, and re-layouts  8.26 us (2%)
  other arithmetic  6.37 us (1%)
    reduce_scatter x1, waiting for transfers between devices, body(): lax.psum_scatter(jnp.stack(pieces, 1).reshape(channels // lax.axis_size('...  158 us
    psum x1, waiting for transfers between devices, body(): kernel_grad = lax.psum(owned, ('tm', 'width'))  147 us
    dot_general x27, matrix products, body(): jnp.dot(block, kernel[:, tap_t, tap_h, tap_w, :], preferred_element_type=...  33.4 us
    dot_general x27, matrix products, body(): lax.dot_general(scaled, block, (((0,), (0,)), ((), ())), preferred_elemen...  30.3 us
    ppermute x4, starting transfers between devices, with_halo(): after = lax.ppermute(initial, axis, down)  12.1 us
    ppermute x4, starting transfers between devices, with_halo(): before = lax.ppermute(last, axis, up)  9.18 us
  transfers between devices with their start and end apart: 12, of which 6 were waited for; matrix products, arithmetic and copies ran while one was open for 8% of the time, Pallas kernels for 0%

commit v1 on v0

v1 whole, which is shorter than its diff:
```python
import functools

import jax
import jax.numpy as jnp
from jax import lax
from jax.experimental import pallas as pl
from jax.experimental.pallas import tpu as pltpu
from jax.sharding import PartitionSpec as P

VMEM_LIMIT = 48 * 1024 * 1024


def shifted(value, axis, by):
    length = lax.axis_size(axis)
    pairs = [(i, i + by) for i in range(length) if 0 <= i + by < length]
    return lax.ppermute(value, axis, pairs)


def with_halo(value, axis, dim):
    length = value.shape[dim]
    before = shifted(lax.slice_in_dim(value, length - 1, length, axis=dim), axis, 1)
    after = shifted(lax.slice_in_dim(value, 0, 1, axis=dim), axis, -1)
    return jnp.concatenate([before, value, after], axis=dim)


def column_taps(padded, columns):
    return jnp.stack([padded[:, :, c : c + columns] for c in range(3)], 0)


def full_spec(shape):
    return pl.BlockSpec(shape, lambda *_: (0,) * len(shape), pipeline_mode=pl.Buffered(1))


def forward_kernel(rows, columns, taps_ref, kernel_ref, bias_ref, cot_ref, dec_ref, sc_ref, acc):
    step = pl.program_id(0)
    tap_t, tap_h = step // 3, step % 3
    channels = acc.shape[1]
    total = None
    for c in range(3):
        block = taps_ref[c, pl.ds(tap_t, 2), pl.ds(tap_h, rows)].reshape(-1, channels)
        part = lax.dot_general(
            block, kernel_ref[c], (((1,), (1,)), ((), ())), preferred_element_type=jnp.float32
        )
        total = part if total is None else total + part

    @pl.when(step == 0)
    def _():
        acc[...] = total + bias_ref[...]

    @pl.when(step > 0)
    def _():
        acc[...] += total

    @pl.when(step == 8)
    def _():
        pre = acc[...]
        sigma = jax.nn.sigmoid(pre)
        dec_ref[...] = (pre * sigma).astype(jnp.bfloat16)
        cot = cot_ref[...].astype(jnp.float32)
        sc_ref[...] = (cot * sigma * (1.0 + pre * (1.0 - sigma))).astype(jnp.bfloat16)


def forward(taps, kernel, bias, cotangent):
    _, _, rows, columns, channels = taps.shape
    rows -= 2
    count = 2 * rows * columns
    flat = jax.ShapeDtypeStruct((count, channels), jnp.bfloat16)
    return pl.pallas_call(
        functools.partial(forward_kernel, rows, columns),
        grid=(9,),
        in_specs=[
            full_spec(taps.shape),
            pl.BlockSpec((3, channels, channels), lambda s: (s, 0, 0)),
            full_spec((1, channels)),
            full_spec((count, channels)),
        ],
        out_specs=[full_spec((count, channels))] * 2,
        out_shape=[flat, flat],
        scratch_shapes=[pltpu.VMEM((count, channels), jnp.float32)],
        compiler_params=pltpu.CompilerParams(vmem_limit_bytes=VMEM_LIMIT),
        cost_estimate=pl.CostEstimate(
            flops=54 * count * channels * channels,
            bytes_accessed=54 * channels * channels,
            transcendentals=count * channels,
        ),
        name="conv_forward",
    )(taps, kernel, bias, cotangent)


def data_kernel(rows, columns, taps_ref, kernel_ref, part_ref):
    step = pl.program_id(0)
    tap_t, tap_h = step // 3, step % 3
    count, channels = rows * columns, part_ref.shape[-1]
    total = None
    for c in range(3):
        block = taps_ref[2 - c, :, pl.ds(2 - tap_h, rows)].reshape(-1, channels)
        part = jnp.dot(block, kernel_ref[c], preferred_element_type=jnp.float32)
        total = part if total is None else total + part

    @pl.when(step == 0)
    def _():
        part_ref[...] = jnp.zeros_like(part_ref)

    part_ref[pl.ds(tap_t, 2)] += total.reshape(2, count, channels)


def data_grad(taps, kernel):
    _, _, rows, columns, channels = taps.shape
    rows -= 2
    shape = (4, rows * columns, channels)
    return pl.pallas_call(
        functools.partial(data_kernel, rows, columns),
        grid=(9,),
        in_specs=[
            full_spec(taps.shape),
            pl.BlockSpec((3, channels, channels), lambda s: (s, 0, 0)),
        ],
        out_specs=full_spec(shape),
        out_shape=jax.ShapeDtypeStruct(shape, jnp.float32),
        compiler_params=pltpu.CompilerParams(vmem_limit_bytes=VMEM_LIMIT),
        cost_estimate=pl.CostEstimate(
            flops=108 * rows * columns * channels * channels,
            bytes_accessed=54 * channels * channels,
            transcendentals=0,
        ),
        name="conv_data_grad",
    )(taps, kernel)


def weight_kernel(rows, taps_ref, scaled_ref, out_ref):
    step = pl.program_id(0)
    tap_t, tap_h = step // 3, step % 3
    channels = out_ref.shape[-1]
    for c in range(3):
        block = taps_ref[c, pl.ds(tap_t, 2), pl.ds(tap_h, rows)].reshape(-1, channels)
        part = jnp.dot(scaled_ref[...], block, preferred_element_type=jnp.float32)
        out_ref[c] = part.astype(out_ref.dtype)


def weight_grad(taps, scaled_t):
    _, _, rows, columns, channels = taps.shape
    rows -= 2
    owned = scaled_t.shape[0]
    return pl.pallas_call(
        functools.partial(weight_kernel, rows),
        grid=(9,),
        in_specs=[full_spec(taps.shape), full_spec(scaled_t.shape)],
        out_specs=pl.BlockSpec((3, owned, channels), lambda s: (s, 0, 0)),
        out_shape=jax.ShapeDtypeStruct((27, owned, channels), jnp.bfloat16),
        compiler_params=pltpu.CompilerParams(vmem_limit_bytes=VMEM_LIMIT),
        cost_estimate=pl.CostEstimate(
            flops=108 * rows * columns * owned * channels,
            bytes_accessed=54 * owned * channels,
            transcendentals=0,
        ),
        name="conv_weight_grad",
    )(taps, scaled_t)


def body(frames, cache_in, kernel, conv_bias, cotangent):
    _, rows, columns, channels = frames.shape
    heights = lax.axis_size("height")
    place = lax.axis_index("height")
    taps_kernel = kernel.transpose(1, 2, 3, 0, 4).reshape(27, channels, channels)

    earlier = shifted(frames, "tm", 1)
    earlier = jnp.where(lax.axis_index("tm") == 0, cache_in, earlier)
    stacked = jnp.concatenate([earlier, frames], 0)
    extended = with_halo(with_halo(stacked, "height", 1), "width", 2)
    taps = column_taps(extended, columns)
    decoded, scaled = forward(
        taps, taps_kernel, conv_bias.reshape(1, channels), cotangent.reshape(-1, channels)
    )
    scaled4 = scaled.reshape(frames.shape)

    if heights == 2:
        half = channels // 2
        inner = extended[:, 1 : rows + 1]
        swap = [(0, 1), (1, 0)]
        other = lax.ppermute(inner, "height", swap)
        edge = jnp.zeros((4, 1) + inner.shape[2:], inner.dtype)
        both = jnp.where(
            place == 0,
            jnp.concatenate([edge, inner, other, edge], 1),
            jnp.concatenate([edge, other, inner, edge], 1),
        )
        all_taps = column_taps(both, columns)
        parts = scaled4[..., :half], scaled4[..., half:]
        mine = jnp.where(place == 0, parts[0], parts[1])
        theirs = jnp.where(place == 0, parts[1], parts[0])
        got = lax.ppermute(theirs, "height", swap)
        joint = jnp.where(
            place == 0, jnp.concatenate([mine, got], 1), jnp.concatenate([got, mine], 1)
        )
        owned = weight_grad(all_taps, joint.reshape(-1, half).T)
    else:
        owned = weight_grad(taps, scaled.T)
        owned = lax.psum_scatter(owned, "height", scatter_dimension=1, tiled=True)
    summed = lax.psum(owned, ("tm", "width")).astype(jnp.float32)
    kernel_grad = summed.reshape(3, 3, 3, -1, channels).transpose(3, 0, 1, 2, 4)

    grad_taps = column_taps(with_halo(with_halo(scaled4, "height", 1), "width", 2), columns)
    partial = data_grad(grad_taps, taps_kernel).reshape(4, rows, columns, channels)
    cache_grad = partial[:2].astype(jnp.bfloat16)
    carried = shifted(cache_grad, "tm", -1)
    frame_grad = (partial[2:] + carried.astype(jnp.float32)).astype(jnp.bfloat16)
    return decoded.reshape(frames.shape), frame_grad, cache_grad, kernel_grad


def solution(mesh):
    split = P("tm", "height", "width", None)
    in_specs = (split, P(None, "height", "width", None), P(), P(), split)
    out_specs = (split, split, split, P("height", None, None, None, None))
    return jax.shard_map(body, mesh=mesh, in_specs=in_specs, out_specs=out_specs, check_vma=False)
```

time: 441 us -> 185 us (0.42)
  waiting for transfers between devices: 311 us -> 92.7 us
  matrix products: 72.3 us -> 0 us
  Pallas kernels: 0 us -> 24.6 us
  starting transfers between devices: 25.3 us -> 38.1 us
  local copies, waits for them, and re-layouts: 8.26 us -> 1.64 us
    reduce_scatter x1 -> x0, waiting for transfers between devices: 158 us -> none  [body(): lax.psum_scatter(jnp.stack(pieces, 1).reshape(channels // lax.axis_size('...]
    dot_general x81 -> x0, matrix products: 72.3 us -> none  [the longest x27 33.4 us: body(): jnp.dot(block, kernel[:, tap_t, tap_h, tap_w, :], preferred_element_type=...]
    psum x1, waiting for transfers between devices: 147 us -> 77.7 us  [body(): summed = lax.psum(owned, ('tm', 'width')).astype(jnp.float32)]
    ppermute x2 -> x10, starting transfers between devices: 3.88 us -> 36 us  [shifted(): return lax.ppermute(value, axis, pairs)]
    pallas_call x0 -> x3, Pallas kernels: none -> 24.6 us  [the longest x1 9.64 us: forward(): pl.pallas_call(functools.partial(forward_kernel, rows, columns), grid=(9,...]
    ppermute x8 -> x2, starting transfers between devices: 21.3 us -> 1.97 us  [the longest x1 1.89 us: body(): other = lax.ppermute(inner, 'height', swap)]
    ppermute x2 -> x10, waiting for transfers between devices: 2.41 us -> 11.2 us  [shifted(): return lax.ppermute(value, axis, pairs)]
    unnamed x13 -> x8, local copies, waits for them, and re-layouts: 7.41 us -> 0.69 us
  transfers between devices with their start and end apart: 12 -> 13, of which waited for: 6 -> 9; matrix products, arithmetic and copies ran while one was open for 8% -> 1% of each run, Pallas kernels for 0% -> 10%
where the time goes in v1:
time: 185 us; the launch traced here: 182 us
  waiting for transfers between devices  92.7 us (50%)
  starting transfers between devices  38.1 us (21%)
  Pallas kernels  24.6 us (13%)
  between operations  14.3 us (8%)
  other arithmetic  10.3 us (6%)
    psum x1, waiting for transfers between devices, body(): summed = lax.psum(owned, ('tm', 'width')).astype(jnp.float32)  77.7 us
    ppermute x10, starting transfers between devices, shifted(): return lax.ppermute(value, axis, pairs)  36 us
    ppermute x10, waiting for transfers between devices, shifted(): return lax.ppermute(value, axis, pairs)  11.2 us
    pallas_call x1, Pallas kernels, forward(): pl.pallas_call(functools.partial(forward_kernel, rows, columns), grid=(9,...  9.64 us
    pallas_call x1, Pallas kernels, data_grad(): pl.pallas_call(functools.partial(data_kernel, rows, columns), grid=(9,),...  8.78 us
    transpose x1, other arithmetic, body(): kernel_grad = summed.reshape(3, 3, 3, -1, channels).transpose(3, 0, 1, 2, 4)  6.33 us
    pallas_call x1, Pallas kernels, weight_grad(): pl.pallas_call(functools.partial(weight_kernel, rows), grid=(9,), in_spec...  6.18 us
    ppermute x1, waiting for transfers between devices, body(): got = lax.ppermute(theirs, 'height', swap)  3.8 us
  transfers between devices with their start and end apart: 13, of which 9 were waited for; matrix products, arithmetic and copies ran while one was open for 1% of the time, Pallas kernels for 10%

profile of v1, /device:TPU:15, one launch (start us, length us, event | category | flops | bytes accessed | tf_op | source)
XLA Modules:
  0.0 181.6 jit_solution(5808910529341963355)
XLA Ops:
  7.2 0.0 copy-start.1
  7.2 0.0 all-reduce.2.cloned.1.call-start
  7.2 1.4 collective-permute-start
  8.7 0.0 copy-start.3
  8.7 2.4 %collective-permute-done = bf16[2,4,32,384]{3,2,1,0:T(8,128)(2,1)S(1)} collective-permute-done((bf16[2,4,32,384]{3,2,1,0:T(8,128)(2,1)}, bf16[2,4,32,384]{3,2,1,0:T(8,128)(2,1)S(1)}, u32[]{:S(2)}, u32[]{:S(2)}) %collective-permute-start) | collective-permute-done | bytes 196640 | tf_op jit(solution)/shard_map/ppermute | solution.py:16
  11.1 0.9 pad_maximum_fusion.29
  12.0 1.3 collective-permute-start.1
  13.3 4.0 %collective-permute-start.2 = (bf16[4,1,32,384]{3,2,1,0:T(8,128)(2,1)S(1)}, bf16[4,1,32,384]{3,2,1,0:T(8,128)(2,1)S(1)}, u32[]{:S(2)}, u32[]{:S(2)}) collective-permute-start(bf16[4,1,32,384]{3,2,1,0:T(8,128)(2,1)S(1)} %get-tuple-element.17), channel_id=1, source_target_pairs={{4,0},{5,1},{6,2},{7,3},{12,8},{13,9},{14,10},{15,11},{20,16},{21,... | collective-permute-start | bytes 294920 | tf_op jit(solution)/shard_map/ppermute | solution.py:16
  17.3 0.1 collective-permute-done.1
  17.3 1.6 collective-permute-done.2
  18.9 0.0 copy-done.1
  18.9 0.1 pad_maximum_fusion.15
  19.0 0.1 fusion.9
  19.1 3.2 %collective-permute-start.3 = (bf16[4,6,1,384]{3,2,1,0:T(2,128)(2,1)S(1)}, bf16[4,6,1,384]{3,2,1,0:T(2,128)(2,1)S(1)}, u32[]{:S(2)}, u32[]{:S(2)}) collective-permute-start(bf16[4,6,1,384]{3,2,1,0:T(2,128)(2,1)S(1)} %get-tuple-element.14), channel_id=1, source_target_pairs={{0,1},{1,2},{2,3},{4,5},{5,6},{6,7},{8,9},{9,10},{10,11},{12,13},{... | collective-permute-start | bytes 55304 | tf_op jit(solution)/shard_map/ppermute | solution.py:16
  22.3 2.1 %collective-permute-start.4 = (bf16[4,6,1,384]{3,2,1,0:T(2,128)(2,1)S(1)}, bf16[4,6,1,384]{3,2,1,0:T(2,128)(2,1)S(1)}, u32[]{:S(2)}, u32[]{:S(2)}) collective-permute-start(bf16[4,6,1,384]{3,2,1,0:T(2,128)(2,1)S(1)} %get-tuple-element.15), channel_id=1, source_target_pairs={{1,0},{2,1},{3,2},{5,4},{6,5},{7,6},{9,8},{10,9},{11,10},{13,12},{... | collective-permute-start | bytes 55304 | tf_op jit(solution)/shard_map/ppermute | solution.py:16
  24.4 0.0 copy-done.3
  24.4 0.0 collective-permute-done.3
  24.4 2.6 %collective-permute-done.4 = bf16[4,6,1,384]{3,2,1,0:T(2,128)(2,1)S(1)} collective-permute-done((bf16[4,6,1,384]{3,2,1,0:T(2,128)(2,1)S(1)}, bf16[4,6,1,384]{3,2,1,0:T(2,128)(2,1)S(1)}, u32[]{:S(2)}, u32[]{:S(2)}) %collective-permute-start.4) | collective-permute-done | bytes 18464 | tf_op jit(solution)/shard_map/ppermute | solution.py:16
  27.0 0.2 pad_maximum_fusion.16
  27.2 1.9 %collective-permute-start.10 = (bf16[4,4,34,384]{3,2,1,0:T(8,128)(2,1)S(1)}, bf16[4,4,34,384]{3,2,1,0:T(8,128)(2,1)S(1)}, u32[]{:S(2)}, u32[]{:S(2)}) collective-permute-start(bf16[4,4,34,384]{3,2,1,0:T(8,128)(2,1)S(1)} %pad_maximum_fusion.16), channel_id=1, source_target_pairs={{0,4},{4,0},{1,5},{5,1},{2,6},{6,2},{3,7},{7,3},{8,12},{12,8},{9,1... | collective-permute-start | bytes 1253384 | tf_op jit(solution)/shard_map/ppermute | solution.py:180
  29.1 0.5 fusion.4
  29.6 0.0 copy-start
  29.6 0.2 pad_maximum_fusion.1.taps_ref
  29.8 0.7 copy-done
  30.5 9.6 %conv_forward.1 = (bf16[256,384]{1,0:T(8,128)(2,1)}, bf16[256,384]{1,0:T(8,128)(2,1)S(1)}) custom-call(bf16[3,4,6,32,384]{4,3,2,1,0:T(8,128)(2,1)S(1)} %pad_maximum_fusion.1.taps_ref, bf16[27,384,384]{2,1,0:T(8,128)(2,1)} %bitcast.37, f32[1,384]{1,0:T(1,128)S(1)} %reshape.37.bias_ref, bf16[256,384]{1,0:T(8,128)(2,1)S(1)} %bitcast.36), custom_call_target="tpu_custom_call" | custom-call | flops 2038431744 | bytes 7962624 | tf_op jit(solution)/shard_map/conv_forward/pallas_call | solution.py:68
  40.2 0.1 broadcast_select_fusion.2
  40.3 0.1 collective-permute-start.11
  40.4 3.8 %collective-permute-done.11 = bf16[2,4,32,192]{3,2,1,0:T(8,128)(2,1)S(1)} collective-permute-done((bf16[2,4,32,192]{3,2,1,0:T(8,128)(2,1)S(1)}, bf16[2,4,32,192]{3,2,1,0:T(8,128)(2,1)S(1)}, u32[]{:S(2)}, u32[]{:S(2)}) %collective-permute-start.11) | collective-permute-done | bytes 98336 | tf_op jit(solution)/shard_map/ppermute | solution.py:191
  44.2 0.1 maximum_select_fusion
  44.3 0.1 copy.10
  44.4 0.0 collective-permute-done.10
  44.4 0.4 fusion.2
  44.8 0.6 slice_bitcast_fusion.2
  45.4 0.4 pad_maximum_fusion.taps_ref
  45.8 6.2 %conv_weight_grad.1 = bf16[27,192,384]{2,1,0:T(8,128)(2,1)} custom-call(bf16[3,4,10,32,384]{4,3,2,1,0:T(8,128)(2,1)S(1)} %pad_maximum_fusion.taps_ref, bf16[192,512]{1,0:T(8,128)(2,1)S(1)} %bitcast.35), custom_call_target="tpu_custom_call" | custom-call | flops 2038431744 | bytes 3981312 | tf_op jit(solution)/shard_map/conv_weight_grad/pallas_call | solution.py:144
  52.0 0.0 all-reduce.2.cloned.1.call-update
  52.1 1.3 collective-permute-start.5
  53.4 4.0 %collective-permute-start.6 = (bf16[2,1,32,384]{3,2,1,0:T(8,128)(2,1)S(1)}, bf16[2,1,32,384]{3,2,1,0:T(8,128)(2,1)S(1)}, u32[]{:S(2)}, u32[]{:S(2)}) collective-permute-start(bf16[2,1,32,384]{3,2,1,0:T(8,128)(2,1)S(1)} %get-tuple-element.26), channel_id=1, source_target_pairs={{4,0},{5,1},{6,2},{7,3},{12,8},{13,9},{14,10},{15,11},{20,16},{21,... | collective-permute-start | bytes 147464 | tf_op jit(solution)/shard_map/ppermute | solution.py:16
  57.4 0.0 collective-permute-done.5
  57.4 1.1 collective-permute-done.6
  58.6 3.2 %collective-permute-start.7 = (bf16[2,6,1,384]{3,2,1,0:T(2,128)(2,1)S(1)}, bf16[2,6,1,384]{3,2,1,0:T(2,128)(2,1)S(1)}, u32[]{:S(2)}, u32[]{:S(2)}) collective-permute-start(bf16[2,6,1,384]{3,2,1,0:T(2,128)(2,1)S(1)} %get-tuple-element.21), channel_id=1, source_target_pairs={{0,1},{1,2},{2,3},{4,5},{5,6},{6,7},{8,9},{9,10},{10,11},{12,13},{... | collective-permute-start | bytes 27656 | tf_op jit(solution)/shard_map/ppermute | solution.py:16
  61.8 2.1 %collective-permute-start.8 = (bf16[2,6,1,384]{3,2,1,0:T(2,128)(2,1)S(1)}, bf16[2,6,1,384]{3,2,1,0:T(2,128)(2,1)S(1)}, u32[]{:S(2)}, u32[]{:S(2)}) collective-permute-start(bf16[2,6,1,384]{3,2,1,0:T(2,128)(2,1)S(1)} %get-tuple-element.22), channel_id=1, source_target_pairs={{1,0},{2,1},{3,2},{5,4},{6,5},{7,6},{9,8},{10,9},{11,10},{13,12},{... | collective-permute-start | bytes 27656 | tf_op jit(solution)/shard_map/ppermute | solution.py:16
  63.9 0.0 collective-permute-done.7
  63.9 2.4 %collective-permute-done.8 = bf16[2,6,1,384]{3,2,1,0:T(2,128)(2,1)S(1)} collective-permute-done((bf16[2,6,1,384]{3,2,1,0:T(2,128)(2,1)S(1)}, bf16[2,6,1,384]{3,2,1,0:T(2,128)(2,1)S(1)}, u32[]{:S(2)}, u32[]{:S(2)}) %collective-permute-start.8) | collective-permute-done | bytes 9248 | tf_op jit(solution)/shard_map/ppermute | solution.py:16
  66.3 0.2 fusion.6
  66.5 0.1 pad_maximum_fusion.6.taps_ref
  66.7 8.8 %conv_data_grad.1 = f32[4,128,384]{2,1,0:T(8,128)S(1)} custom-call(bf16[3,2,6,32,384]{4,3,2,1,0:T(8,128)(2,1)S(1)} %pad_maximum_fusion.6.taps_ref, bf16[27,384,384]{2,1,0:T(8,128)(2,1)} %bitcast.38), custom_call_target="tpu_custom_call" | custom-call | flops 2038431744 | bytes 7962624 | tf_op jit(solution)/shard_map/conv_data_grad/pallas_call | solution.py:111
  75.5 0.0 copy-start.2
  75.5 13.5 %collective-permute-start.9 = (bf16[2,4,32,384]{3,2,1,0:T(8,128)(2,1)S(1)}, bf16[2,4,32,384]{3,2,1,0:T(8,128)(2,1)S(1)}, u32[]{:S(2)}, u32[]{:S(2)}) collective-permute-start(bf16[2,4,32,384]{3,2,1,0:T(8,128)(2,1)S(1)} %bitcast.42), channel_id=1, source_target_pairs={{8,0},{16,8},{24,16},{9,1},{17,9},{25,17},{10,2},{18,10},{26,18},{... | collective-permute-start | bytes 589832 | tf_op jit(solution)/shard_map/ppermute | solution.py:16
  89.0 1.0 collective-permute-done.9
  90.0 0.7 add_convert_fusion
  90.8 77.7 %all-reduce.2.cloned.1.call-done = bf16[192,3,3,3,384]{4,0,3,2,1:T(8,128)(2,1)} async-done(((bf16[192,3,3,3,384]{4,0,3,2,1:T(8,128)(2,1)}), bf16[192,3,3,3,384]{4,0,3,2,1:T(8,128)(2,1)}) %all-reduce.2.cloned.1.call-update) | async-done | bytes 3981328 | tf_op jit(solution)/shard_map/psum | solution.py:199
  168.4 6.3 %transpose.15 = f32[192,3,3,3,384]{4,0,3,2,1:T(8,128)} convert(bf16[192,3,3,3,384]{4,0,3,2,1:T(8,128)(2,1)} %all-reduce.2.cloned.1.call-done) | non-fusion elementwise | flops 1990656 | bytes 11943936 | tf_op jit(solution)/shard_map/transpose | solution.py:200
  174.8 0.0 copy-done.2
  (8 shorter events, 0.2 us)
Async XLA Ops:
  7.2 11.7 %copy-start.1 = (bf16[2,4,32,384]{3,2,1,0:T(8,128)(2,1)S(1)}, bf16[2,4,32,384]{3,2,1,0:T(8,128)(2,1)}, u32[]{:S(2)}) copy-start(bf16[2,4,32,384]{3,2,1,0:T(8,128)(2,1)} %param.5) | copy-start | bytes 589828
  7.2 161.3 %all-reduce.2.cloned.1.call-start = ((), (), s32[]{:S(2)}) async-start(), calls=%async_computation | async-start | bytes 7962624 | tf_op jit(solution)/shard_map/psum | solution.py:199
  7.2 3.9 %collective-permute-start = (bf16[2,4,32,384]{3,2,1,0:T(8,128)(2,1)}, bf16[2,4,32,384]{3,2,1,0:T(8,128)(2,1)S(1)}, u32[]{:S(2)}, u32[]{:S(2)}) collective-permute-start(bf16[2,4,32,384]{3,2,1,0:T(8,128)(2,1)} %param.5), channel_id=1, source_target_pairs={{0,8},{8,16},{16,24},{1,9},{9,17},{17,25},{2,10},{10,18},{18,26},{... | collective-permute-start | bytes 589832 | tf_op jit(solution)/shard_map/ppermute | solution.py:16
  8.7 15.7 %copy-start.3 = (f32[384]{0:T(512)S(1)}, f32[384]{0:T(512)}, u32[]{:S(2)}) copy-start(f32[384]{0:T(512)} %param.8) | copy-start | bytes 4612
  12.0 5.4 %collective-permute-start.1 = (bf16[4,1,32,384]{3,2,1,0:T(8,128)(2,1)S(1)}, bf16[4,1,32,384]{3,2,1,0:T(8,128)(2,1)S(1)}, u32[]{:S(2)}, u32[]{:S(2)}) collective-permute-start(bf16[4,1,32,384]{3,2,1,0:T(8,128)(2,1)S(1)} %get-tuple-element.16), channel_id=1, source_target_pairs={{0,4},{1,5},{2,6},{3,7},{8,12},{9,13},{10,14},{11,15},{16,20},{17,... | collective-permute-start | bytes 294920 | tf_op jit(solution)/shard_map/ppermute | solution.py:16
  13.3 5.6 %collective-permute-start.2 = (bf16[4,1,32,384]{3,2,1,0:T(8,128)(2,1)S(1)}, bf16[4,1,32,384]{3,2,1,0:T(8,128)(2,1)S(1)}, u32[]{:S(2)}, u32[]{:S(2)}) collective-permute-start(bf16[4,1,32,384]{3,2,1,0:T(8,128)(2,1)S(1)} %get-tuple-element.17), channel_id=1, source_target_pairs={{4,0},{5,1},{6,2},{7,3},{12,8},{13,9},{14,10},{15,11},{20,16},{21,... | collective-permute-start | bytes 294920 | tf_op jit(solution)/shard_map/ppermute | solution.py:16
  19.1 5.3 %collective-permute-start.3 = (bf16[4,6,1,384]{3,2,1,0:T(2,128)(2,1)S(1)}, bf16[4,6,1,384]{3,2,1,0:T(2,128)(2,1)S(1)}, u32[]{:S(2)}, u32[]{:S(2)}) collective-permute-start(bf16[4,6,1,384]{3,2,1,0:T(2,128)(2,1)S(1)} %get-tuple-element.14), channel_id=1, source_target_pairs={{0,1},{1,2},{2,3},{4,5},{5,6},{6,7},{8,9},{9,10},{10,11},{12,13},{... | collective-permute-start | bytes 55304 | tf_op jit(solution)/shard_map/ppermute | solution.py:16
  22.3 4.7 %collective-permute-start.4 = (bf16[4,6,1,384]{3,2,1,0:T(2,128)(2,1)S(1)}, bf16[4,6,1,384]{3,2,1,0:T(2,128)(2,1)S(1)}, u32[]{:S(2)}, u32[]{:S(2)}) collective-permute-start(bf16[4,6,1,384]{3,2,1,0:T(2,128)(2,1)S(1)} %get-tuple-element.15), channel_id=1, source_target_pairs={{1,0},{2,1},{3,2},{5,4},{6,5},{7,6},{9,8},{10,9},{11,10},{13,12},{... | collective-permute-start | bytes 55304 | tf_op jit(solution)/shard_map/ppermute | solution.py:16
  27.2 17.2 %collective-permute-start.10 = (bf16[4,4,34,384]{3,2,1,0:T(8,128)(2,1)S(1)}, bf16[4,4,34,384]{3,2,1,0:T(8,128)(2,1)S(1)}, u32[]{:S(2)}, u32[]{:S(2)}) collective-permute-start(bf16[4,4,34,384]{3,2,1,0:T(8,128)(2,1)S(1)} %pad_maximum_fusion.16), channel_id=1, source_target_pairs={{0,4},{4,0},{1,5},{5,1},{2,6},{6,2},{3,7},{7,3},{8,12},{12,8},{9,1... | collective-permute-start | bytes 1253384 | tf_op jit(solution)/shard_map/ppermute | solution.py:180
  29.6 0.9 copy-start
  40.3 3.9 %collective-permute-start.11 = (bf16[2,4,32,192]{3,2,1,0:T(8,128)(2,1)S(1)}, bf16[2,4,32,192]{3,2,1,0:T(8,128)(2,1)S(1)}, u32[]{:S(2)}, u32[]{:S(2)}) collective-permute-start(bf16[2,4,32,192]{3,2,1,0:T(8,128)(2,1)S(1)} %get-tuple-element.24), channel_id=1, source_target_pairs={{0,4},{4,0},{1,5},{5,1},{2,6},{6,2},{3,7},{7,3},{8,12},{12,8},{9,1... | collective-permute-start | bytes 294920 | tf_op jit(solution)/shard_map/ppermute | solution.py:191
  52.1 5.3 %collective-permute-start.5 = (bf16[2,1,32,384]{3,2,1,0:T(8,128)(2,1)S(1)}, bf16[2,1,32,384]{3,2,1,0:T(8,128)(2,1)S(1)}, u32[]{:S(2)}, u32[]{:S(2)}) collective-permute-start(bf16[2,1,32,384]{3,2,1,0:T(8,128)(2,1)S(1)} %get-tuple-element.25), channel_id=1, source_target_pairs={{0,4},{1,5},{2,6},{3,7},{8,12},{9,13},{10,14},{11,15},{16,20},{17,... | collective-permute-start | bytes 147464 | tf_op jit(solution)/shard_map/ppermute | solution.py:16
  53.4 5.2 %collective-permute-start.6 = (bf16[2,1,32,384]{3,2,1,0:T(8,128)(2,1)S(1)}, bf16[2,1,32,384]{3,2,1,0:T(8,128)(2,1)S(1)}, u32[]{:S(2)}, u32[]{:S(2)}) collective-permute-start(bf16[2,1,32,384]{3,2,1,0:T(8,128)(2,1)S(1)} %get-tuple-element.26), channel_id=1, source_target_pairs={{4,0},{5,1},{6,2},{7,3},{12,8},{13,9},{14,10},{15,11},{20,16},{21,... | collective-permute-start | bytes 147464 | tf_op jit(solution)/shard_map/ppermute | solution.py:16
  58.6 5.3 %collective-permute-start.7 = (bf16[2,6,1,384]{3,2,1,0:T(2,128)(2,1)S(1)}, bf16[2,6,1,384]{3,2,1,0:T(2,128)(2,1)S(1)}, u32[]{:S(2)}, u32[]{:S(2)}) collective-permute-start(bf16[2,6,1,384]{3,2,1,0:T(2,128)(2,1)S(1)} %get-tuple-element.21), channel_id=1, source_target_pairs={{0,1},{1,2},{2,3},{4,5},{5,6},{6,7},{8,9},{9,10},{10,11},{12,13},{... | collective-permute-start | bytes 27656 | tf_op jit(solution)/shard_map/ppermute | solution.py:16
  61.8 4.5 %collective-permute-start.8 = (bf16[2,6,1,384]{3,2,1,0:T(2,128)(2,1)S(1)}, bf16[2,6,1,384]{3,2,1,0:T(2,128)(2,1)S(1)}, u32[]{:S(2)}, u32[]{:S(2)}) collective-permute-start(bf16[2,6,1,384]{3,2,1,0:T(2,128)(2,1)S(1)} %get-tuple-element.22), channel_id=1, source_target_pairs={{1,0},{2,1},{3,2},{5,4},{6,5},{7,6},{9,8},{10,9},{11,10},{13,12},{... | collective-permute-start | bytes 27656 | tf_op jit(solution)/shard_map/ppermute | solution.py:16
  75.5 99.3 %copy-start.2 = (bf16[2,128,384]{2,1,0:T(8,128)(2,1)}, bf16[2,128,384]{2,1,0:T(8,128)(2,1)S(1)}, u32[]{:S(2)}) copy-start(bf16[2,128,384]{2,1,0:T(8,128)(2,1)S(1)} %slice.111) | copy-start | bytes 589828
  75.5 14.5 %collective-permute-start.9 = (bf16[2,4,32,384]{3,2,1,0:T(8,128)(2,1)S(1)}, bf16[2,4,32,384]{3,2,1,0:T(8,128)(2,1)S(1)}, u32[]{:S(2)}, u32[]{:S(2)}) collective-permute-start(bf16[2,4,32,384]{3,2,1,0:T(8,128)(2,1)S(1)} %bitcast.42), channel_id=1, source_target_pairs={{8,0},{16,8},{24,16},{9,1},{17,9},{25,17},{10,2},{18,10},{26,18},{... | collective-permute-start | bytes 589832 | tf_op jit(solution)/shard_map/ppermute | solution.py:16
Sparse Core Ops, SparseCore 0:
  52.2 116.2 all-reduce.1

commit v2 on v1

--- a/solution.py
+++ b/solution.py
@@ -31,13 +31,18 @@
     return pl.BlockSpec(shape, lambda *_: (0,) * len(shape), pipeline_mode=pl.Buffered(1))
 
 
-def forward_kernel(rows, columns, taps_ref, kernel_ref, bias_ref, cot_ref, dec_ref, sc_ref, acc):
+def first_row(paired, rows):
+    return lax.axis_index("height") * rows if paired else 0
+
+
+def forward_kernel(rows, paired, taps_ref, kernel_ref, bias_ref, cot_ref, dec_ref, sc_ref, acc):
     step = pl.program_id(0)
     tap_t, tap_h = step // 3, step % 3
     channels = acc.shape[1]
+    start = first_row(paired, rows)
     total = None
     for c in range(3):
-        block = taps_ref[c, pl.ds(tap_t, 2), pl.ds(tap_h, rows)].reshape(-1, channels)
+        block = taps_ref[c, pl.ds(tap_t, 2), pl.ds(start + tap_h, rows)].reshape(-1, channels)
         part = lax.dot_general(
             block, kernel_ref[c], (((1,), (1,)), ((), ())), preferred_element_type=jnp.float32
         )
@@ -60,13 +65,12 @@
         sc_ref[...] = (cot * sigma * (1.0 + pre * (1.0 - sigma))).astype(jnp.bfloat16)
 
 
-def forward(taps, kernel, bias, cotangent):
-    _, _, rows, columns, channels = taps.shape
-    rows -= 2
+def forward(taps, kernel, bias, cotangent, rows, paired):
+    _, _, _, columns, channels = taps.shape
     count = 2 * rows * columns
     flat = jax.ShapeDtypeStruct((count, channels), jnp.bfloat16)
     return pl.pallas_call(
-        functools.partial(forward_kernel, rows, columns),
+        functools.partial(forward_kernel, rows, paired),
         grid=(9,),
         in_specs=[
             full_spec(taps.shape),
@@ -87,13 +91,14 @@
     )(taps, kernel, bias, cotangent)
 
 
-def data_kernel(rows, columns, taps_ref, kernel_ref, part_ref):
+def data_kernel(rows, columns, paired, taps_ref, kernel_ref, part_ref):
     step = pl.program_id(0)
     tap_t, tap_h = step // 3, step % 3
     count, channels = rows * columns, part_ref.shape[-1]
+    start = first_row(paired, rows)
     total = None
     for c in range(3):
-        block = taps_ref[2 - c, :, pl.ds(2 - tap_h, rows)].reshape(-1, channels)
+        block = taps_ref[2 - c, :, pl.ds(start + 2 - tap_h, rows)].reshape(-1, channels)
         part = jnp.dot(block, kernel_ref[c], preferred_element_type=jnp.float32)
         total = part if total is None else total + part
 
@@ -104,12 +109,11 @@
     part_ref[pl.ds(tap_t, 2)] += total.reshape(2, count, channels)
 
 
-def data_grad(taps, kernel):
-    _, _, rows, columns, channels = taps.shape
-    rows -= 2
+def data_grad(taps, kernel, rows, paired):
+    _, _, _, columns, channels = taps.shape
     shape = (4, rows * columns, channels)
     return pl.pallas_call(
-        functools.partial(data_kernel, rows, columns),
+        functools.partial(data_kernel, rows, columns, paired),
         grid=(9,),
         in_specs=[
             full_spec(taps.shape),
@@ -157,50 +161,157 @@
     )(taps, scaled_t)
 
 
-def body(frames, cache_in, kernel, conv_bias, cotangent):
-    _, rows, columns, channels = frames.shape
-    heights = lax.axis_size("height")
+def exchange_kernel(depth, *refs):
+    sources, edges = refs[:depth], refs[depth : 2 * depth]
+    main_ref, edge_ref, send_sem, recv_sem = refs[2 * depth :]
+    mesh_id = pl.DeviceIdType.MESH
+    k, h, w = (lax.axis_index(axis) for axis in ("tm", "height", "width"))
+    times, widths = lax.axis_size("tm"), lax.axis_size("width")
+    left, right = lax.rem(w + widths - 1, widths), lax.rem(w + 1, widths)
+
+    barrier = pltpu.get_barrier_semaphore()
+    count = 0
+    for slot in range(2 * depth):
+        dk, dh = slot // 2, slot % 2
+        sender = lax.rem(k + times - dk, times), (1 - h if dh else h)
+        for column in (left, right) + ((w,) if slot else ()):
+            pl.semaphore_signal(
+                barrier, inc=1, device_id=sender + (column,), device_id_type=mesh_id
+            )
+            count += 1
+    pl.semaphore_wait(barrier, count)
+
+    copies = []
+    for slot in range(2 * depth):
+        dk, dh = slot // 2, slot % 2
+        target = lax.rem(k + dk, times), (1 - h if dh else h)
+        plan = [(edges[dk].at[0], edge_ref.at[slot, 0], left)]
+        plan.append((edges[dk].at[1], edge_ref.at[slot, 1], right))
+        if slot:
+            plan.append((sources[dk], main_ref.at[slot - 1], w))
+        for source, place, column in plan:
+            index = len(copies)
+            copy = pltpu.make_async_remote_copy(
+                src_ref=source,
+                dst_ref=place,
+                send_sem=send_sem.at[index],
+                recv_sem=recv_sem.at[index],
+                device_id=target + (column,),
+                device_id_type=mesh_id,
+            )
+            copy.start()
+            copies.append(copy)
+    for copy in copies:
+        copy.wait()
+
+
+def exchange(sources, collective_id):
+    depth = len(sources)
+    shape = sources[0].shape
+    channels = shape[-1]
+    rim = shape[0] * shape[1]
+    padded = -(-rim // 16) * 16
+
+    def columns_of(value):
+        ends = jnp.stack([value[:, :, 0], value[:, :, -1]], 0).reshape(2, rim, channels)
+        return jnp.pad(ends, ((0, 0), (0, padded - rim), (0, 0)))
+
+    edges = [columns_of(value) for value in sources]
+    copies = 6 * depth - 1
+    vmem = pl.BlockSpec(memory_space=pltpu.VMEM)
+    main, ends = pl.pallas_call(
+        functools.partial(exchange_kernel, depth),
+        in_specs=[vmem] * (2 * depth),
+        out_specs=[vmem] * 2,
+        out_shape=[
+            jax.ShapeDtypeStruct((2 * depth - 1,) + shape, jnp.bfloat16),
+            jax.ShapeDtypeStruct((2 * depth, 2, padded, channels), jnp.bfloat16),
+        ],
+        scratch_shapes=[pltpu.SemaphoreType.DMA((copies,)), pltpu.SemaphoreType.DMA((copies,))],
+        compiler_params=pltpu.CompilerParams(collective_id=collective_id, has_side_effects=True),
+        name="exchange_%d" % depth,
+    )(*sources, *edges)
+    ends = ends[:, :, :rim].reshape(2 * depth, 2, shape[0], shape[1], 1, channels)
+    return main, ends
+
+
+def join_rows(mine, other, ends_mine, ends_other):
+    place, column = lax.axis_index("height"), lax.axis_index("width")
+    last = lax.axis_size("width") - 1
+
+    def wide(value, ends):
+        before = jnp.where(column == 0, jnp.zeros_like(ends[1]), ends[1])
+        after = jnp.where(column == last, jnp.zeros_like(ends[0]), ends[0])
+        return jnp.concatenate([before, value, after], 2)
+
+    mine, other = wide(mine, ends_mine), wide(other, ends_other)
+    edge = jnp.zeros_like(mine[:, :1])
+    return jnp.where(
+        place == 0,
+        jnp.concatenate([edge, mine, other, edge], 1),
+        jnp.concatenate([edge, other, mine, edge], 1),
+    )
+
+
+def reduce_weights(owned):
+    return lax.psum(owned, ("tm", "width")).astype(jnp.float32)
+
+
+def paired_rows(frames, cache_in, kernel, bias, cotangent):
+    rows, columns, channels = frames.shape[1:]
     place = lax.axis_index("height")
-    taps_kernel = kernel.transpose(1, 2, 3, 0, 4).reshape(27, channels, channels)
-
+    is_last = lax.axis_index("tm") == lax.axis_size("tm") - 1
+    onward = jnp.where(is_last, cache_in, frames)
+    main, ends = exchange([frames, onward], 0)
+    both = join_rows(
+        jnp.concatenate([main[1], frames], 0),
+        jnp.concatenate([main[2], main[0]], 0),
+        jnp.concatenate([ends[2], ends[0]], 1),
+        jnp.concatenate([ends[3], ends[1]], 1),
+    )
+    taps = column_taps(both, columns)
+    decoded, scaled = forward(taps, kernel, bias, cotangent, rows, True)
+
+    mine = scaled.reshape(frames.shape)
+    main, ends = exchange([mine], 1)
+    other = main[0]
+    half = channels // 2
+    upper, lower = jnp.where(place == 0, mine, other), jnp.where(place == 0, other, mine)
+    joint = jnp.concatenate([upper, lower], 1).reshape(-1, channels)
+    joint = jnp.where(place == 0, joint[:, :half], joint[:, half:])
+    summed = reduce_weights(weight_grad(taps, joint.T))
+    grad_taps = column_taps(join_rows(mine, other, ends[0], ends[1]), columns)
+    return decoded, summed, data_grad(grad_taps, kernel, rows, True)
+
+
+def single_rows(frames, cache_in, kernel, bias, cotangent):
+    rows, columns, _ = frames.shape[1:]
     earlier = shifted(frames, "tm", 1)
     earlier = jnp.where(lax.axis_index("tm") == 0, cache_in, earlier)
     stacked = jnp.concatenate([earlier, frames], 0)
-    extended = with_halo(with_halo(stacked, "height", 1), "width", 2)
-    taps = column_taps(extended, columns)
-    decoded, scaled = forward(
-        taps, taps_kernel, conv_bias.reshape(1, channels), cotangent.reshape(-1, channels)
+    taps = column_taps(with_halo(with_halo(stacked, "height", 1), "width", 2), columns)
+    decoded, scaled = forward(taps, kernel, bias, cotangent, rows, False)
+    owned = lax.psum_scatter(
+        weight_grad(taps, scaled.T), "height", scatter_dimension=1, tiled=True
     )
     scaled4 = scaled.reshape(frames.shape)
-
-    if heights == 2:
-        half = channels // 2
-        inner = extended[:, 1 : rows + 1]
-        swap = [(0, 1), (1, 0)]
-        other = lax.ppermute(inner, "height", swap)
-        edge = jnp.zeros((4, 1) + inner.shape[2:], inner.dtype)
-        both = jnp.where(
-            place == 0,
-            jnp.concatenate([edge, inner, other, edge], 1),
-            jnp.concatenate([edge, other, inner, edge], 1),
-        )
-        all_taps = column_taps(both, columns)
-        parts = scaled4[..., :half], scaled4[..., half:]
-        mine = jnp.where(place == 0, parts[0], parts[1])
-        theirs = jnp.where(place == 0, parts[1], parts[0])
-        got = lax.ppermute(theirs, "height", swap)
-        joint = jnp.where(
-            place == 0, jnp.concatenate([mine, got], 1), jnp.concatenate([got, mine], 1)
-        )
-        owned = weight_grad(all_taps, joint.reshape(-1, half).T)
-    else:
-        owned = weight_grad(taps, scaled.T)
-        owned = lax.psum_scatter(owned, "height", scatter_dimension=1, tiled=True)
-    summed = lax.psum(owned, ("tm", "width")).astype(jnp.float32)
+    grad_taps = column_taps(with_halo(with_halo(scaled4, "height", 1), "width", 2), columns)
+    return decoded, reduce_weights(owned), data_grad(grad_taps, kernel, rows, False)
+
+
+def body(frames, cache_in, kernel, conv_bias, cotangent):
+    _, rows, columns, channels = frames.shape
+    taps_kernel = kernel.transpose(1, 2, 3, 0, 4).reshape(27, channels, channels)
+    run = paired_rows if lax.axis_size("height") == 2 else single_rows
+    decoded, summed, partial = run(
+        frames,
+        cache_in,
+        taps_kernel,
+        conv_bias.reshape(1, channels),
+        cotangent.reshape(-1, channels),
+    )
     kernel_grad = summed.reshape(3, 3, 3, -1, channels).transpose(3, 0, 1, 2, 4)
-
-    grad_taps = column_taps(with_halo(with_halo(scaled4, "height", 1), "width", 2), columns)
-    partial = data_grad(grad_taps, taps_kernel).reshape(4, rows, columns, channels)
+    partial = partial.reshape(4, rows, columns, channels)
     cache_grad = partial[:2].astype(jnp.bfloat16)
     carried = shifted(cache_grad, "tm", -1)
     frame_grad = (partial[2:] + carried.astype(jnp.float32)).astype(jnp.bfloat16)

time: 185 us -> 186 us (level)
  starting transfers between devices: 38.1 us -> 2.11 us
  Pallas kernels: 24.6 us -> 49.8 us
  local copies, waits for them, and re-layouts: 1.64 us -> 7.51 us
  other arithmetic: 10.3 us -> 13.5 us
  waiting for transfers between devices: 92.7 us -> 95.1 us
    ppermute x10 -> x1, starting transfers between devices: 36 us -> 2.07 us  [shifted(): return lax.ppermute(value, axis, pairs)]
    pallas_call x2 -> x4, Pallas kernels: 18.4 us -> 43.6 us  [the longest x2 25.1 us: exchange(): pl.pallas_call(functools.partial(exchange_kernel, depth), in_specs=[vmem]...]
    psum x1, waiting for transfers between devices: 77.7 us -> 94 us  [reduce_weights(): return lax.psum(owned, ('tm', 'width')).astype(jnp.float32)]
    ppermute x10 -> x1, waiting for transfers between devices: 11.2 us -> 1.01 us  [shifted(): return lax.ppermute(value, axis, pairs)]
    ppermute x2 -> x0, waiting for transfers between devices: 3.8 us -> none  [the longest x1 3.8 us: body(): got = lax.ppermute(theirs, 'height', swap)]
    select_n x4 -> x7, other arithmetic: 0.59 us -> 3.66 us  [the longest x2 1.53 us: join_rows(): jnp.where(place == 0, jnp.concatenate([edge, mine, other, edge], 1), jnp....]
    ppermute x2 -> x0, starting transfers between devices: 1.97 us -> none  [the longest x1 1.89 us: body(): other = lax.ppermute(inner, 'height', swap)]
  transfers between devices with their start and end apart: 13 -> 2, of which waited for: 9 -> 2; matrix products, arithmetic and copies ran while one was open for 1% -> 1% of each run, Pallas kernels for 10% -> 5%
where the time goes in v2:
time: 186 us; the launch traced here: 182 us
  waiting for transfers between devices  95.1 us (51%)
  Pallas kernels  49.8 us (27%)
  between operations  14.3 us (8%)
  other arithmetic  13.5 us (7%)
  local copies, waits for them, and re-layouts  7.51 us (4%)
  starting transfers between devices  2.11 us (1%)
    psum x1, waiting for transfers between devices, reduce_weights(): return lax.psum(owned, ('tm', 'width')).astype(jnp.float32)  94 us
    pallas_call x2, Pallas kernels, exchange(): pl.pallas_call(functools.partial(exchange_kernel, depth), in_specs=[vmem]...  25.1 us
    pallas_call x1, Pallas kernels, forward(): pl.pallas_call(functools.partial(forward_kernel, rows, paired), grid=(9,)...  9.64 us
    pallas_call x1, Pallas kernels, data_grad(): pl.pallas_call(functools.partial(data_kernel, rows, columns, paired), gri...  8.82 us
    transpose x1, other arithmetic, body(): kernel_grad = summed.reshape(3, 3, 3, -1, channels).transpose(3, 0, 1, 2, 4)  6.33 us
    pallas_call x1, Pallas kernels, weight_grad(): pl.pallas_call(functools.partial(weight_kernel, rows), grid=(9,), in_spec...  6.2 us
  transfers between devices with their start and end apart: 2, of which 2 were waited for; matrix products, arithmetic and copies ran while one was open for 1% of the time, Pallas kernels for 5%

profile of v2, /device:TPU:15, one launch (start us, length us, event | category | flops | bytes accessed | tf_op | source)
XLA Modules:
  0.0 182.3 jit_solution(10096392325390162769)
XLA Ops:
  7.2 0.0 all-reduce.5.cloned.1.call-start
  7.2 0.7 reshape.192.bias_ref
  7.9 0.9 slice_reduce_fusion.5
  8.8 0.0 copy-start.3
  8.8 1.0 broadcast_select_fusion.2.refs_1_
  9.9 0.0 copy-start.4
  9.9 0.1 slice_reduce_fusion.3
  10.0 0.6 fusion.12
  10.6 0.0 copy-done.4
  10.6 15.5 %exchange_2.1 = (bf16[3,2,4,32,384]{4,3,2,1,0:T(8,128)(2,1)}, bf16[4,2,16,384]{3,2,1,0:T(8,128)(2,1)}) custom-call(bf16[2,4,32,384]{3,2,1,0:T(8,128)(2,1)} %refs_0_.1, bf16[2,4,32,384]{3,2,1,0:T(8,128)(2,1)} %copy-done.4, bf16[2,16,384]{2,1,0:T(8,128)(2,1)} %get-tuple-element.47.refs_2_, bf16[2,16,384]{2,1,0:T(8,128)(2,1)} %get-tuple-element.48.refs_3_), custom_call_target="tpu_custom_call" | custom-call | tf_op jit(solution)/shard_map/exchange_2/pallas_call | solution.py:222
  26.1 0.8 fusion.26
  27.1 1.2 slice_bitcast_fusion.8
  28.4 0.0 copy-done.3
  28.4 1.2 fusion.2
  29.6 0.6 slice_bitcast_fusion.2
  30.2 0.0 copy-start.2
  30.2 0.4 pad_maximum_fusion.taps_ref
  30.6 0.5 copy-done.2
  31.2 9.6 %conv_forward.1 = (bf16[256,384]{1,0:T(8,128)(2,1)}, bf16[256,384]{1,0:T(8,128)(2,1)S(1)}) custom-call(bf16[3,4,10,32,384]{4,3,2,1,0:T(8,128)(2,1)S(1)} %pad_maximum_fusion.taps_ref, bf16[27,384,384]{2,1,0:T(8,128)(2,1)} %bitcast.69, f32[1,384]{1,0:T(1,128)S(1)} %reshape.192.bias_ref, bf16[256,384]{1,0:T(8,128)(2,1)S(1)} %bitcast.68), custom_call_target="tpu_custom_call" | custom-call | flops 2038431744 | bytes 7962624 | tf_op jit(solution)/shard_map/conv_forward/pallas_call | solution.py:72
  40.8 0.0 copy-start
  40.8 0.1 slice_reduce_fusion.1
  40.9 0.6 fusion.14.refs_1_
  41.5 0.0 copy-done
  41.5 9.6 %exchange_1.1 = (bf16[1,2,4,32,384]{4,3,2,1,0:T(8,128)(2,1)}, bf16[2,2,16,384]{3,2,1,0:T(8,128)(2,1)}) custom-call(bf16[2,4,32,384]{3,2,1,0:T(8,128)(2,1)} %bitcast.66, bf16[2,16,384]{2,1,0:T(8,128)(2,1)} %fusion.14.refs_1_), custom_call_target="tpu_custom_call" | custom-call | tf_op jit(solution)/shard_map/exchange_1/pallas_call | solution.py:222
  51.1 1.1 broadcast_select_fusion.1
  52.2 0.1 fusion.25
  52.4 0.8 copy.61
  53.2 0.1 copy.60
  53.3 1.0 select_bitcast_fusion.scaled_ref
  54.3 6.2 %conv_weight_grad.1 = bf16[27,192,384]{2,1,0:T(8,128)(2,1)} custom-call(bf16[3,4,10,32,384]{4,3,2,1,0:T(8,128)(2,1)S(1)} %pad_maximum_fusion.taps_ref, bf16[192,512]{1,0:T(8,128)(2,1)S(1)} %select_bitcast_fusion.scaled_ref), custom_call_target="tpu_custom_call" | custom-call | flops 2038431744 | bytes 3981312 | tf_op jit(solution)/shard_map/conv_weight_grad/pallas_call | solution.py:148
  60.5 0.0 copy-start.7
  60.5 0.0 copy-start.1
  60.5 0.0 copy-start.5
  60.5 0.0 all-reduce.5.cloned.1.call-update
  60.5 0.8 copy-done.7
  61.4 0.1 copy-done.1
  61.5 0.1 copy-done.5
  61.5 0.3 fusion.5
  61.9 0.3 slice_bitcast_fusion.5
  62.2 0.2 pad_maximum_fusion.5.taps_ref
  62.4 8.8 %conv_data_grad.1 = f32[4,128,384]{2,1,0:T(8,128)S(1)} custom-call(bf16[3,2,10,32,384]{4,3,2,1,0:T(8,128)(2,1)S(1)} %pad_maximum_fusion.5.taps_ref, bf16[27,384,384]{2,1,0:T(8,128)(2,1)} %bitcast.70), custom_call_target="tpu_custom_call" | custom-call | flops 2038431744 | bytes 7962624 | tf_op jit(solution)/shard_map/conv_data_grad/pallas_call | solution.py:115
  71.2 0.0 copy-start.6
  71.2 2.1 %collective-permute-start = (bf16[2,4,32,384]{3,2,1,0:T(8,128)(2,1)S(1)}, bf16[2,4,32,384]{3,2,1,0:T(8,128)(2,1)S(1)}, u32[]{:S(2)}, u32[]{:S(2)}) collective-permute-start(bf16[2,4,32,384]{3,2,1,0:T(8,128)(2,1)S(1)} %bitcast.75), channel_id=1, source_target_pairs={{8,0},{16,8},{24,16},{9,1},{17,9},{25,17},{10,2},{18,10},{26,18},{... | collective-permute-start | bytes 589832 | tf_op jit(solution)/shard_map/ppermute | solution.py:16
  73.4 1.0 collective-permute-done
  74.4 0.7 add_convert_fusion
  75.1 94.0 %all-reduce.5.cloned.1.call-done = bf16[192,3,3,3,384]{4,0,3,2,1:T(8,128)(2,1)} async-done(((bf16[192,3,3,3,384]{4,0,3,2,1:T(8,128)(2,1)}), bf16[192,3,3,3,384]{4,0,3,2,1:T(8,128)(2,1)}) %all-reduce.5.cloned.1.call-update) | async-done | bytes 3981328 | tf_op jit(solution)/shard_map/psum | solution.py:257
  169.1 6.3 %transpose.15 = f32[192,3,3,3,384]{4,0,3,2,1:T(8,128)} convert(bf16[192,3,3,3,384]{4,0,3,2,1:T(8,128)(2,1)} %all-reduce.5.cloned.1.call-done) | non-fusion elementwise | flops 1990656 | bytes 11943936 | tf_op jit(solution)/shard_map/transpose | solution.py:313
  175.5 0.0 copy-done.6
  (26 shorter events, 0.4 us)
Async XLA Ops:
  7.2 162.0 %all-reduce.5.cloned.1.call-start = ((), (), s32[]{:S(2)}) async-start(), calls=%async_computation | async-start | bytes 7962624 | tf_op jit(solution)/shard_map/psum | solution.py:257
  8.8 19.5 %copy-start.3 = (bf16[2,4,32,384]{3,2,1,0:T(8,128)(2,1)S(1)}, bf16[2,4,32,384]{3,2,1,0:T(8,128)(2,1)}, u32[]{:S(2)}) copy-start(bf16[2,4,32,384]{3,2,1,0:T(8,128)(2,1)} %refs_0_.1) | copy-start | bytes 589828
  9.9 0.7 copy-start.4
  30.2 0.9 copy-start.2
  40.8 0.7 copy-start
  60.5 0.8 copy-start.7
  60.5 1.0 copy-start.1
  60.5 1.0 copy-start.5
  71.2 104.2 %copy-start.6 = (bf16[2,128,384]{2,1,0:T(8,128)(2,1)}, bf16[2,128,384]{2,1,0:T(8,128)(2,1)S(1)}, u32[]{:S(2)}) copy-start(bf16[2,128,384]{2,1,0:T(8,128)(2,1)S(1)} %slice.216) | copy-start | bytes 589828
  71.2 3.1 %collective-permute-start = (bf16[2,4,32,384]{3,2,1,0:T(8,128)(2,1)S(1)}, bf16[2,4,32,384]{3,2,1,0:T(8,128)(2,1)S(1)}, u32[]{:S(2)}, u32[]{:S(2)}) collective-permute-start(bf16[2,4,32,384]{3,2,1,0:T(8,128)(2,1)S(1)} %bitcast.75), channel_id=1, source_target_pairs={{8,0},{16,8},{24,16},{9,1},{17,9},{25,17},{10,2},{18,10},{26,18},{... | collective-permute-start | bytes 589832 | tf_op jit(solution)/shard_map/ppermute | solution.py:16
Sparse Core Ops, SparseCore 0:
  60.6 108.4 all-reduce.4

commit v3 on v2

--- a/solution.py
+++ b/solution.py
@@ -8,6 +8,7 @@
 from jax.sharding import PartitionSpec as P
 
 VMEM_LIMIT = 48 * 1024 * 1024
+CHUNKS = 3
 
 
 def shifted(value, axis, by):
@@ -150,7 +151,7 @@
         grid=(9,),
         in_specs=[full_spec(taps.shape), full_spec(scaled_t.shape)],
         out_specs=pl.BlockSpec((3, owned, channels), lambda s: (s, 0, 0)),
-        out_shape=jax.ShapeDtypeStruct((27, owned, channels), jnp.bfloat16),
+        out_shape=jax.ShapeDtypeStruct((28, owned, channels), jnp.bfloat16),
         compiler_params=pltpu.CompilerParams(vmem_limit_bytes=VMEM_LIMIT),
         cost_estimate=pl.CostEstimate(
             flops=108 * rows * columns * owned * channels,
@@ -253,6 +254,124 @@
     )
 
 
+def sum_kernel(widths, in_ref, out_ref, got1, sent2, got2, sent3, got3, whole, send_sem, recv_sem):
+    size = in_ref.shape[0] // CHUNKS
+    half, quarter = size // 2, size // 4
+    piece = quarter // widths
+    mesh_id = pl.DeviceIdType.MESH
+    k, h, w = (lax.axis_index(axis) for axis in ("tm", "height", "width"))
+    core, chip = lax.rem(k, 2), k // 2
+    core_mate = (k + 1 - 2 * core, h, w)
+    chip_mate = (lax.rem(k + 2, 4), h, w)
+    line = [(k, h, lax.rem(w + d, widths)) for d in range(1, widths)]
+    f32, bf16 = jnp.float32, jnp.bfloat16
+
+    barrier = pltpu.get_barrier_semaphore()
+    for mate in [core_mate, chip_mate] + line:
+        pl.semaphore_signal(barrier, inc=1, device_id=mate, device_id_type=mesh_id)
+    pl.semaphore_wait(barrier, 1 + widths)
+
+    def rows(start, count):
+        return pl.ds(pl.multiple_of(start, 16), count)
+
+    used = []
+
+    def send(source, place, mate):
+        index = len(used)
+        used.append(index)
+        copy = pltpu.make_async_remote_copy(
+            src_ref=source,
+            dst_ref=place,
+            send_sem=send_sem.at[index],
+            recv_sem=recv_sem.at[index],
+            device_id=mate,
+            device_id_type=mesh_id,
+        )
+        copy.start()
+        return copy
+
+    base = [c * size for c in range(CHUNKS)]
+    own_half = [b + core * half for b in base]
+    own_quarter = [b + chip * quarter for b in own_half]
+    own_piece = [b + w * piece for b in own_quarter]
+
+    first = [
+        send(in_ref.at[rows(base[c] + (1 - core) * half, half)], got1.at[c], core_mate)
+        for c in range(CHUNKS)
+    ]
+    second, third, fourth, fifth, sixth = [], [], [], [], []
+    for c in range(CHUNKS):
+        first[c].wait()
+        away = (1 - chip) * quarter
+        mine = in_ref[rows(own_half[c] + away, quarter)].astype(f32)
+        sent2[c] = (mine + got1[c, rows(away, quarter)].astype(f32)).astype(bf16)
+        second.append(send(sent2.at[c], got2.at[c], chip_mate))
+    for c in range(CHUNKS):
+        second[c].wait()
+        mine = in_ref[rows(own_quarter[c], quarter)].astype(f32)
+        mine = mine + got1[c, rows(chip * quarter, quarter)].astype(f32)
+        sent3[c] = (mine + got2[c].astype(f32)).astype(bf16)
+        third.append(
+            [
+                send(sent3.at[c, rows(mate[2] * piece, piece)], got3.at[c, d], mate)
+                for d, mate in enumerate(line)
+            ]
+        )
+    for c in range(CHUNKS):
+        total = in_ref[rows(own_piece[c], piece)].astype(f32)
+        total = total + got1[c, rows(chip * quarter + w * piece, piece)].astype(f32)
+        total = total + got2[c, rows(w * piece, piece)].astype(f32)
+        for d, copy in enumerate(third[c]):
+            copy.wait()
+            total = total + got3[c, d].astype(f32)
+        whole[rows(own_piece[c], piece)] = total.astype(bf16)
+        place = whole.at[rows(own_piece[c], piece)]
+        fourth.append([send(place, place, mate) for mate in line])
+    for c in range(CHUNKS):
+        for copy in fourth[c]:
+            copy.wait()
+        place = whole.at[rows(own_quarter[c], quarter)]
+        fifth.append(send(place, place, chip_mate))
+    for c in range(CHUNKS):
+        fifth[c].wait()
+        place = whole.at[rows(own_half[c], half)]
+        sixth.append(send(place, place, core_mate))
+    for c in range(CHUNKS):
+        sixth[c].wait()
+        stop = min(base[c] + size, out_ref.shape[0])
+        out_ref[base[c] : stop] = whole[base[c] : stop].astype(f32)
+
+
+def sum_blocks(local, valid):
+    total, channels = local.shape
+    widths = lax.axis_size("width")
+    size = total // CHUNKS
+    half, quarter = size // 2, size // 4
+    copies = CHUNKS * (4 + 2 * (widths - 1))
+    bf16 = jnp.bfloat16
+    vmem = pl.BlockSpec(memory_space=pltpu.VMEM)
+    return pl.pallas_call(
+        functools.partial(sum_kernel, widths),
+        in_specs=[vmem],
+        out_specs=vmem,
+        out_shape=jax.ShapeDtypeStruct((valid, channels), jnp.float32),
+        scratch_shapes=[
+            pltpu.VMEM((CHUNKS, half, channels), bf16),
+            pltpu.VMEM((CHUNKS, quarter, channels), bf16),
+            pltpu.VMEM((CHUNKS, quarter, channels), bf16),
+            pltpu.VMEM((CHUNKS, quarter, channels), bf16),
+            pltpu.VMEM((CHUNKS, widths - 1, quarter // widths, channels), bf16),
+            pltpu.VMEM((total, channels), bf16),
+            pltpu.SemaphoreType.DMA((copies,)),
+            pltpu.SemaphoreType.DMA((copies,)),
+        ],
+        compiler_params=pltpu.CompilerParams(
+            collective_id=2, has_side_effects=True, vmem_limit_bytes=VMEM_LIMIT
+        ),
+        name="sum_blocks",
+    )(local)
+
+
 def reduce_weights(owned):
     return lax.psum(owned, ("tm", "width")).astype(jnp.float32)
 
@@ -279,7 +398,12 @@
     upper, lower = jnp.where(place == 0, mine, other), jnp.where(place == 0, other, mine)
     joint = jnp.concatenate([upper, lower], 1).reshape(-1, channels)
     joint = jnp.where(place == 0, joint[:, :half], joint[:, half:])
-    summed = reduce_weights(weight_grad(taps, joint.T))
+    local = weight_grad(taps, joint.T)
+    unit = 16 * 4 * lax.axis_size("width") * CHUNKS
+    if lax.axis_size("tm") == 4 and 28 * half % unit == 0:
+        summed = sum_blocks(local.reshape(28 * half, channels), 27 * half)
+    else:
+        summed = reduce_weights(local[:27])
     grad_taps = column_taps(join_rows(mine, other, ends[0], ends[1]), columns)
     return decoded, summed, data_grad(grad_taps, kernel, rows, True)
 
@@ -292,7 +416,7 @@
     taps = column_taps(with_halo(with_halo(stacked, "height", 1), "width", 2), columns)
     decoded, scaled = forward(taps, kernel, bias, cotangent, rows, False)
     owned = lax.psum_scatter(
-        weight_grad(taps, scaled.T), "height", scatter_dimension=1, tiled=True
+        weight_grad(taps, scaled.T)[:27], "height", scatter_dimension=1, tiled=True
     )
     scaled4 = scaled.reshape(frames.shape)
     grad_taps = column_taps(with_halo(with_halo(scaled4, "height", 1), "width", 2), columns)

time: 186 us -> 161 us (0.87); the launches traced: 182 us -> 160 us
  waiting for transfers between devices: 95.1 us -> 0.01 us
  Pallas kernels: 49.8 us -> 130 us
  between operations: 14.3 us -> 0.94 us
  local copies, waits for them, and re-layouts: 7.51 us -> 16.8 us
  other arithmetic: 13.5 us -> 9.28 us
    psum x1 -> x0, waiting for transfers between devices: 94 us -> none  [reduce_weights(): return lax.psum(owned, ('tm', 'width')).astype(jnp.float32)]
    pallas_call x0 -> x1, Pallas kernels: none -> 80.3 us  [sum_blocks(): pl.pallas_call(functools.partial(sum_kernel, widths), in_specs=[vmem], ou...]
    unnamed x18 -> x19, local copies, waits for them, and re-layouts: 2.42 us -> 11 us
    transpose x2 -> x1, other arithmetic: 7.29 us -> 0.96 us  [paired_rows(): local = weight_grad(taps, joint.T)]
  transfers between devices with their start and end apart: 2 -> 1, of which waited for: 2 -> 0; matrix products, arithmetic and copies ran while one was open for 1% -> 1% of each run, Pallas kernels for 5% -> 54%
where the time goes in v3:
time: 161 us; the launch traced here: 160 us
  Pallas kernels  130 us (81%)
  local copies, waits for them, and re-layouts  16.8 us (10%)
  other arithmetic  9.28 us (6%)
  starting transfers between devices  2.77 us (2%)
    pallas_call x1, Pallas kernels, sum_blocks(): pl.pallas_call(functools.partial(sum_kernel, widths), in_specs=[vmem], ou...  80.3 us
    pallas_call x2, Pallas kernels, exchange(): pl.pallas_call(functools.partial(exchange_kernel, depth), in_specs=[vmem]...  25.1 us
    unnamed x19, local copies, waits for them, and re-layouts  11 us
    pallas_call x1, Pallas kernels, forward(): pl.pallas_call(functools.partial(forward_kernel, rows, paired), grid=(9,)...  9.64 us
    pallas_call x1, Pallas kernels, data_grad(): pl.pallas_call(functools.partial(data_kernel, rows, columns, paired), gri...  8.76 us
    pallas_call x1, Pallas kernels, weight_grad(): pl.pallas_call(functools.partial(weight_kernel, rows), grid=(9,), in_spec...  6.19 us
  transfers between devices with their start and end apart: 1, of which 0 were waited for; matrix products, arithmetic and copies ran while one was open for 1% of the time, Pallas kernels for 54%

profile of v3, /device:TPU:15, one launch (start us, length us, event | category | flops | bytes accessed | tf_op | source)
XLA Modules:
  0.0 159.8 jit_solution(6093483269903715236)
XLA Ops:
  0.6 0.7 reshape.194.bias_ref
  1.3 0.9 slice_reduce_fusion.5
  2.3 0.0 copy-start.5
  2.3 1.0 broadcast_select_fusion.2.refs_1_
  3.3 0.0 copy-start.6
  3.3 0.1 slice_reduce_fusion.3
  3.4 0.6 fusion.12
  4.0 0.0 copy-done.6
  4.0 15.5 %exchange_2.1 = (bf16[3,2,4,32,384]{4,3,2,1,0:T(8,128)(2,1)}, bf16[4,2,16,384]{3,2,1,0:T(8,128)(2,1)}) custom-call(bf16[2,4,32,384]{3,2,1,0:T(8,128)(2,1)} %refs_0_.1, bf16[2,4,32,384]{3,2,1,0:T(8,128)(2,1)} %copy-done.6, bf16[2,16,384]{2,1,0:T(8,128)(2,1)} %get-tuple-element.47.refs_2_, bf16[2,16,384]{2,1,0:T(8,128)(2,1)} %get-tuple-element.48.refs_3_), custom_call_target="tpu_custom_call" | custom-call | tf_op jit(solution)/shard_map/exchange_2/pallas_call | solution.py:223
  19.6 0.8 fusion.26
  20.6 1.2 slice_bitcast_fusion.8
  21.8 0.0 copy-done.5
  21.8 1.2 fusion.2
  23.0 0.6 slice_bitcast_fusion.2
  23.7 0.0 copy-start.4
  23.7 0.4 pad_maximum_fusion.taps_ref
  24.1 0.5 copy-done.4
  24.6 9.6 %conv_forward.1 = (bf16[256,384]{1,0:T(8,128)(2,1)}, bf16[256,384]{1,0:T(8,128)(2,1)S(1)}) custom-call(bf16[3,4,10,32,384]{4,3,2,1,0:T(8,128)(2,1)S(1)} %pad_maximum_fusion.taps_ref, bf16[27,384,384]{2,1,0:T(8,128)(2,1)} %bitcast.72, f32[1,384]{1,0:T(1,128)S(1)} %reshape.194.bias_ref, bf16[256,384]{1,0:T(8,128)(2,1)S(1)} %bitcast.71), custom_call_target="tpu_custom_call" | custom-call | flops 2038431744 | bytes 7962624 | tf_op jit(solution)/shard_map/conv_forward/pallas_call | solution.py:73
  34.2 0.0 copy-start.2
  34.2 0.1 slice_reduce_fusion.1
  34.3 0.6 fusion.14.refs_1_
  35.0 0.0 copy-done.2
  35.0 9.6 %exchange_1.1 = (bf16[1,2,4,32,384]{4,3,2,1,0:T(8,128)(2,1)}, bf16[2,2,16,384]{3,2,1,0:T(8,128)(2,1)}) custom-call(bf16[2,4,32,384]{3,2,1,0:T(8,128)(2,1)} %bitcast.69, bf16[2,16,384]{2,1,0:T(8,128)(2,1)} %fusion.14.refs_1_), custom_call_target="tpu_custom_call" | custom-call | tf_op jit(solution)/shard_map/exchange_1/pallas_call | solution.py:223
  44.6 0.8 slice_select_fusion.3
  45.4 1.7 %fusion.5 = bf16[2,10,34,384]{3,2,1,0:T(8,128)(2,1)S(1)} fusion(bf16[2,1,34,384]{3,2,1,0:T(8,128)(2,1)S(1)} %broadcast_in_dim.7, bf16[2,4,1,384]{3,2,1,0:T(2,128)(2,1)S(1)} %select_n.208, bf16[2,4,32,384]{3,2,1,0:T(8,128)(2,1)} %bitcast.76, bf16[2,4,1,384]{3,2,1,0:T(2,128)(2,1)S(1)} %select_n.207, bf16[2,4,1,384]{3,2,1,0:T(2,128)(2,1)S(1)} %select_n.206, ...), kind=kLoop, calls=%fused_computation.18 | loop fusion | flops 8094720 | bytes 992257 | tf_op jit(solution)/shard_map/jit(_where)/select_n | solution.py:250
  47.1 0.3 slice_bitcast_fusion.5
  47.4 0.2 pad_maximum_fusion.5.taps_ref
  47.6 0.0 copy-start.3
  47.6 0.0 copy-start.7
  47.6 8.8 %conv_data_grad.1 = f32[4,128,384]{2,1,0:T(8,128)S(1)} custom-call(bf16[3,2,10,32,384]{4,3,2,1,0:T(8,128)(2,1)S(1)} %pad_maximum_fusion.5.taps_ref, bf16[27,384,384]{2,1,0:T(8,128)(2,1)} %bitcast.73), custom_call_target="tpu_custom_call" | custom-call | flops 2038431744 | bytes 7962624 | tf_op jit(solution)/shard_map/conv_data_grad/pallas_call | solution.py:116
  56.4 0.0 copy-start.1
  56.4 0.8 slice.216
  57.2 2.8 %collective-permute-start = (bf16[2,4,32,384]{3,2,1,0:T(8,128)(2,1)}, bf16[2,4,32,384]{3,2,1,0:T(8,128)(2,1)}, u32[]{:S(2)}, u32[]{:S(2)}) collective-permute-start(bf16[2,4,32,384]{3,2,1,0:T(8,128)(2,1)} %bitcast.25), channel_id=1, source_target_pairs={{8,0},{16,8},{24,16},{9,1},{17,9},{25,17},{10,2},{18,10},{26,18},{... | collective-permute-start | bytes 589832 | tf_op jit(solution)/shard_map/ppermute | solution.py:17
  60.0 0.0 copy-done.3
  60.0 0.0 copy-done.7
  60.1 0.1 fusion.25
  60.2 0.0 copy-done.1
  60.2 0.8 copy.61
  61.0 0.1 copy.60
  61.2 1.0 select_bitcast_fusion.scaled_ref
  62.1 6.2 %conv_weight_grad.1 = bf16[28,192,384]{2,1,0:T(8,128)(2,1)} custom-call(bf16[3,4,10,32,384]{4,3,2,1,0:T(8,128)(2,1)S(1)} %pad_maximum_fusion.taps_ref, bf16[192,512]{1,0:T(8,128)(2,1)S(1)} %select_bitcast_fusion.scaled_ref), custom_call_target="tpu_custom_call" | custom-call | flops 2038431744 | bytes 3981312 | tf_op jit(solution)/shard_map/conv_weight_grad/pallas_call | solution.py:149
  68.3 0.0 copy-start
  68.3 2.2 %copy-done = bf16[28,192,384]{2,1,0:T(8,128)(2,1)S(1)} copy-done((bf16[28,192,384]{2,1,0:T(8,128)(2,1)S(1)}, bf16[28,192,384]{2,1,0:T(8,128)(2,1)}, u32[]{:S(2)}) %copy-start) | copy-done | bytes 4128792
  70.5 0.0 slice-start
  70.5 80.3 %sum_blocks.1 = f32[5184,384]{1,0:T(8,128)} custom-call(bf16[5376,384]{1,0:T(8,128)(2,1)S(1)} %bitcast.66), custom_call_target="tpu_custom_call" | custom-call | tf_op jit(solution)/shard_map/sum_blocks/pallas_call | solution.py:353
  150.8 0.0 collective-permute-done
  150.8 0.0 slice-done
  150.8 1.6 %add_convert_fusion = bf16[2,4,32,384]{3,2,1,0:T(8,128)(2,1)} fusion(f32[2,4,32,384]{3,2,1,0:T(8,128)S(1)} %bitcast.67, bf16[2,4,32,384]{3,2,1,0:T(8,128)(2,1)} %collective-permute-done), kind=kLoop, calls=%fused_computation.24 | loop fusion | flops 294912 | bytes 786432 | tf_op jit(solution)/shard_map/convert_element_type | solution.py:441
  152.5 7.4 %copy.63 = f32[192,3,3,3,384]{4,0,3,2,1:T(8,128)} copy(f32[192,3,3,3,384]{4,0,3,2,1:T(8,128)} %bitcast.74) | data formatting | bytes 15925248
  (24 shorter events, 0.4 us)
Async XLA Ops:
  2.3 19.5 %copy-start.5 = (bf16[2,4,32,384]{3,2,1,0:T(8,128)(2,1)S(1)}, bf16[2,4,32,384]{3,2,1,0:T(8,128)(2,1)}, u32[]{:S(2)}) copy-start(bf16[2,4,32,384]{3,2,1,0:T(8,128)(2,1)} %refs_0_.1) | copy-start | bytes 589828
  3.3 0.7 copy-start.6
  23.7 0.9 copy-start.4
  34.2 0.7 copy-start.2
  47.6 12.3 %copy-start.3 = (bf16[256,384]{1,0:T(8,128)(2,1)S(1)}, bf16[256,384]{1,0:T(8,128)(2,1)}, u32[]{:S(2)}) copy-start(bf16[256,384]{1,0:T(8,128)(2,1)} %copy-done.2) | copy-start | bytes 589828
  47.6 12.3 %copy-start.7 = (bf16[1,2,4,32,384]{4,3,2,1,0:T(8,128)(2,1)S(1)}, bf16[1,2,4,32,384]{4,3,2,1,0:T(8,128)(2,1)}, u32[]{:S(2)}) copy-start(bf16[1,2,4,32,384]{4,3,2,1,0:T(8,128)(2,1)} %get-tuple-element.15) | copy-start | bytes 589828
  56.4 3.8 %copy-start.1 = (f32[4,128,384]{2,1,0:T(8,128)}, f32[4,128,384]{2,1,0:T(8,128)S(1)}, u32[]{:S(2)}) copy-start(f32[4,128,384]{2,1,0:T(8,128)S(1)} %conv_data_grad.1) | copy-start | bytes 2359300
  57.2 93.6 %collective-permute-start = (bf16[2,4,32,384]{3,2,1,0:T(8,128)(2,1)}, bf16[2,4,32,384]{3,2,1,0:T(8,128)(2,1)}, u32[]{:S(2)}, u32[]{:S(2)}) collective-permute-start(bf16[2,4,32,384]{3,2,1,0:T(8,128)(2,1)} %bitcast.25), channel_id=1, source_target_pairs={{8,0},{16,8},{24,16},{9,1},{17,9},{25,17},{10,2},{18,10},{26,18},{... | collective-permute-start | bytes 589832 | tf_op jit(solution)/shard_map/ppermute | solution.py:17
  68.3 2.2 %copy-start = (bf16[28,192,384]{2,1,0:T(8,128)(2,1)S(1)}, bf16[28,192,384]{2,1,0:T(8,128)(2,1)}, u32[]{:S(2)}) copy-start(bf16[28,192,384]{2,1,0:T(8,128)(2,1)} %conv_weight_grad.1) | copy-start | bytes 12386308
  70.5 80.3 %slice-start = ((f32[4,128,384]{2,1,0:T(8,128)}), f32[2,128,384]{2,1,0:T(8,128)S(1)}, s32[]{:S(2)}) async-start(f32[4,128,384]{2,1,0:T(8,128)} %copy-done.1), calls=%async_computation | async-start | bytes 786432 | tf_op jit(solution)/shard_map/slice | solution.py:441

commit v4 on v3

--- a/solution.py
+++ b/solution.py
@@ -254,7 +254,7 @@
     )
 
 
-def sum_kernel(widths, in_ref, out_ref, got1, sent2, got2, sent3, got3, whole, send_sem, recv_sem):
+def sum_kernel(widths, in_ref, whole, got1, sent2, got2, sent3, got3, send_sem, recv_sem):
     size = in_ref.shape[0] // CHUNKS
     half, quarter = size // 2, size // 4
     piece = quarter // widths
@@ -338,8 +338,6 @@
         sixth.append(send(place, place, core_mate))
     for c in range(CHUNKS):
         sixth[c].wait()
-        stop = min(base[c] + size, out_ref.shape[0])
-        out_ref[base[c] : stop] = whole[base[c] : stop].astype(f32)
 
 
 def sum_blocks(local, valid):
@@ -350,18 +348,17 @@
     copies = CHUNKS * (4 + 2 * (widths - 1))
     bf16 = jnp.bfloat16
     vmem = pl.BlockSpec(memory_space=pltpu.VMEM)
-    return pl.pallas_call(
+    summed = pl.pallas_call(
         functools.partial(sum_kernel, widths),
         in_specs=[vmem],
         out_specs=vmem,
-        out_shape=jax.ShapeDtypeStruct((valid, channels), jnp.float32),
+        out_shape=jax.ShapeDtypeStruct((total, channels), bf16),
         scratch_shapes=[
             pltpu.VMEM((CHUNKS, half, channels), bf16),
             pltpu.VMEM((CHUNKS, quarter, channels), bf16),
             pltpu.VMEM((CHUNKS, quarter, channels), bf16),
             pltpu.VMEM((CHUNKS, quarter, channels), bf16),
             pltpu.VMEM((CHUNKS, widths - 1, quarter // widths, channels), bf16),
-            pltpu.VMEM((total, channels), bf16),
             pltpu.SemaphoreType.DMA((copies,)),
             pltpu.SemaphoreType.DMA((copies,)),
         ],
@@ -370,6 +367,7 @@
         ),
         name="sum_blocks",
     )(local)
+    return summed[:valid].astype(jnp.float32)
 
 
 def reduce_weights(owned):

time: 161 us -> 155 us (0.963)
  local copies, waits for them, and re-layouts: 16.8 us -> 7.67 us
  other arithmetic: 9.28 us -> 13.5 us
    unnamed x19 -> x16, local copies, waits for them, and re-layouts: 11 us -> 1.48 us
    transpose x0 -> x1, other arithmetic: none -> 4.21 us  [body(): kernel_grad = summed.reshape(3, 3, 3, -1, channels).transpose(3, 0, 1, 2, 4)]
  transfers between devices with their start and end apart: 1 -> 1, of which waited for: 0 -> 0; matrix products, arithmetic and copies ran while one was open for 1% -> 4% of each run, Pallas kernels for 54% -> 56%
where the time goes in v4:
time: 155 us; the launch traced here: 154 us
  Pallas kernels  129 us (83%)
  other arithmetic  13.5 us (9%)
  local copies, waits for them, and re-layouts  7.67 us (5%)
  starting transfers between devices  2.76 us (2%)
    pallas_call x1, Pallas kernels, sum_blocks(): pl.pallas_call(functools.partial(sum_kernel, widths), in_specs=[vmem], ou...  79.3 us
    pallas_call x2, Pallas kernels, exchange(): pl.pallas_call(functools.partial(exchange_kernel, depth), in_specs=[vmem]...  25.2 us
    pallas_call x1, Pallas kernels, forward(): pl.pallas_call(functools.partial(forward_kernel, rows, paired), grid=(9,)...  9.64 us
    pallas_call x1, Pallas kernels, data_grad(): pl.pallas_call(functools.partial(data_kernel, rows, columns, paired), gri...  8.76 us
    pallas_call x1, Pallas kernels, weight_grad(): pl.pallas_call(functools.partial(weight_kernel, rows), grid=(9,), in_spec...  6.18 us
    transpose x1, other arithmetic, body(): kernel_grad = summed.reshape(3, 3, 3, -1, channels).transpose(3, 0, 1, 2, 4)  4.21 us
  transfers between devices with their start and end apart: 1, of which 0 were waited for; matrix products, arithmetic and copies ran while one was open for 4% of the time, Pallas kernels for 56%

profile of v4, /device:TPU:15, one launch (start us, length us, event | category | flops | bytes accessed | tf_op | source)
XLA Modules:
  0.0 153.9 jit_solution(13483917352873524950)
XLA Ops:
  0.6 0.7 reshape.195.bias_ref
  1.3 0.9 slice_reduce_fusion.5
  2.3 0.0 copy-start.4
  2.3 1.0 broadcast_select_fusion.2.refs_1_
  3.3 0.0 copy-start.5
  3.3 0.1 slice_reduce_fusion.3
  3.4 0.6 fusion.12
  4.0 0.0 copy-done.5
  4.0 15.5 %exchange_2.1 = (bf16[3,2,4,32,384]{4,3,2,1,0:T(8,128)(2,1)}, bf16[4,2,16,384]{3,2,1,0:T(8,128)(2,1)}) custom-call(bf16[2,4,32,384]{3,2,1,0:T(8,128)(2,1)} %refs_0_.1, bf16[2,4,32,384]{3,2,1,0:T(8,128)(2,1)} %copy-done.5, bf16[2,16,384]{2,1,0:T(8,128)(2,1)} %get-tuple-element.47.refs_2_, bf16[2,16,384]{2,1,0:T(8,128)(2,1)} %get-tuple-element.48.refs_3_), custom_call_target="tpu_custom_call" | custom-call | tf_op jit(solution)/shard_map/exchange_2/pallas_call | solution.py:223
  19.6 0.8 fusion.26
  20.6 1.2 slice_bitcast_fusion.8
  21.8 0.0 copy-done.4
  21.8 1.2 fusion.2
  23.0 0.6 slice_bitcast_fusion.2
  23.7 0.0 copy-start.3
  23.7 0.4 pad_maximum_fusion.taps_ref
  24.1 0.5 copy-done.3
  24.6 9.6 %conv_forward.1 = (bf16[256,384]{1,0:T(8,128)(2,1)}, bf16[256,384]{1,0:T(8,128)(2,1)S(1)}) custom-call(bf16[3,4,10,32,384]{4,3,2,1,0:T(8,128)(2,1)S(1)} %pad_maximum_fusion.taps_ref, bf16[27,384,384]{2,1,0:T(8,128)(2,1)} %bitcast.72, f32[1,384]{1,0:T(1,128)S(1)} %reshape.195.bias_ref, bf16[256,384]{1,0:T(8,128)(2,1)S(1)} %bitcast.71), custom_call_target="tpu_custom_call" | custom-call | flops 2038431744 | bytes 7962624 | tf_op jit(solution)/shard_map/conv_forward/pallas_call | solution.py:73
  34.3 0.0 copy-start.1
  34.3 0.1 slice_reduce_fusion.1
  34.4 0.6 fusion.14.refs_1_
  35.0 0.0 copy-done.1
  35.0 9.6 %exchange_1.1 = (bf16[1,2,4,32,384]{4,3,2,1,0:T(8,128)(2,1)}, bf16[2,2,16,384]{3,2,1,0:T(8,128)(2,1)}) custom-call(bf16[2,4,32,384]{3,2,1,0:T(8,128)(2,1)} %bitcast.69, bf16[2,16,384]{2,1,0:T(8,128)(2,1)} %fusion.14.refs_1_), custom_call_target="tpu_custom_call" | custom-call | tf_op jit(solution)/shard_map/exchange_1/pallas_call | solution.py:223
  44.6 0.8 slice_select_fusion.3
  45.4 1.7 %fusion.5 = bf16[2,10,34,384]{3,2,1,0:T(8,128)(2,1)S(1)} fusion(bf16[2,1,34,384]{3,2,1,0:T(8,128)(2,1)S(1)} %broadcast_in_dim.7, bf16[2,4,1,384]{3,2,1,0:T(2,128)(2,1)S(1)} %select_n.208, bf16[2,4,32,384]{3,2,1,0:T(8,128)(2,1)} %bitcast.77, bf16[2,4,1,384]{3,2,1,0:T(2,128)(2,1)S(1)} %select_n.207, bf16[2,4,1,384]{3,2,1,0:T(2,128)(2,1)S(1)} %select_n.206, ...), kind=kLoop, calls=%fused_computation.19 | loop fusion | flops 8094720 | bytes 992257 | tf_op jit(solution)/shard_map/jit(_where)/select_n | solution.py:250
  47.2 0.3 slice_bitcast_fusion.5
  47.5 0.2 pad_maximum_fusion.5.taps_ref
  47.7 0.0 copy-start.2
  47.7 0.0 copy-start.6
  47.7 8.8 %conv_data_grad.1 = f32[4,128,384]{2,1,0:T(8,128)S(1)} custom-call(bf16[3,2,10,32,384]{4,3,2,1,0:T(8,128)(2,1)S(1)} %pad_maximum_fusion.5.taps_ref, bf16[27,384,384]{2,1,0:T(8,128)(2,1)} %bitcast.73), custom_call_target="tpu_custom_call" | custom-call | flops 2038431744 | bytes 7962624 | tf_op jit(solution)/shard_map/conv_data_grad/pallas_call | solution.py:116
  56.5 0.0 copy-start
  56.5 0.8 slice.220
  57.2 2.8 %collective-permute-start = (bf16[2,4,32,384]{3,2,1,0:T(8,128)(2,1)}, bf16[2,4,32,384]{3,2,1,0:T(8,128)(2,1)}, u32[]{:S(2)}, u32[]{:S(2)}) collective-permute-start(bf16[2,4,32,384]{3,2,1,0:T(8,128)(2,1)} %bitcast.25), channel_id=1, source_target_pairs={{8,0},{16,8},{24,16},{9,1},{17,9},{25,17},{10,2},{18,10},{26,18},{... | collective-permute-start | bytes 589832 | tf_op jit(solution)/shard_map/ppermute | solution.py:17
  60.0 0.0 copy-done.2
  60.0 0.0 copy-done.6
  60.1 0.1 fusion.25
  60.2 0.0 copy-done
  60.2 0.8 copy.61
  61.0 0.1 copy.60
  61.2 1.0 select_bitcast_fusion.scaled_ref
  62.1 6.2 %conv_weight_grad.1 = bf16[28,192,384]{2,1,0:T(8,128)(2,1)} custom-call(bf16[3,4,10,32,384]{4,3,2,1,0:T(8,128)(2,1)S(1)} %pad_maximum_fusion.taps_ref, bf16[192,512]{1,0:T(8,128)(2,1)S(1)} %select_bitcast_fusion.scaled_ref), custom_call_target="tpu_custom_call" | custom-call | flops 2038431744 | bytes 3981312 | tf_op jit(solution)/shard_map/conv_weight_grad/pallas_call | solution.py:149
  68.3 79.3 %sum_blocks.1 = bf16[5376,384]{1,0:T(8,128)(2,1)S(1)} custom-call(bf16[5376,384]{1,0:T(8,128)(2,1)} %bitcast.75), custom_call_target="tpu_custom_call" | custom-call | tf_op jit(solution)/shard_map/sum_blocks/pallas_call | solution.py:351
  147.6 0.4 slice.157
  148.0 0.0 slice-start
  148.0 4.2 %convert_bitcast_fusion = f32[192,3,3,3,384]{4,0,3,2,1:T(8,128)} fusion(bf16[3,3,3,192,384]{4,3,2,1,0:T(8,128)(2,1)S(1)} %bitcast.74), kind=kLoop, calls=%fused_computation | loop fusion | flops 1990656 | bytes 11943936 | tf_op jit(solution)/shard_map/transpose | solution.py:435
  152.2 0.0 collective-permute-done
  152.2 0.0 slice-done
  152.2 1.7 %add_convert_fusion = bf16[2,4,32,384]{3,2,1,0:T(8,128)(2,1)} fusion(f32[2,4,32,384]{3,2,1,0:T(8,128)S(1)} %bitcast.67, bf16[2,4,32,384]{3,2,1,0:T(8,128)(2,1)} %collective-permute-done), kind=kLoop, calls=%fused_computation.25 | loop fusion | flops 294912 | bytes 786432 | tf_op jit(solution)/shard_map/convert_element_type | solution.py:439
  (24 shorter events, 0.4 us)
Async XLA Ops:
  2.3 19.5 %copy-start.4 = (bf16[2,4,32,384]{3,2,1,0:T(8,128)(2,1)S(1)}, bf16[2,4,32,384]{3,2,1,0:T(8,128)(2,1)}, u32[]{:S(2)}) copy-start(bf16[2,4,32,384]{3,2,1,0:T(8,128)(2,1)} %refs_0_.1) | copy-start | bytes 589828
  3.3 0.8 copy-start.5
  23.7 0.9 copy-start.3
  34.3 0.7 copy-start.1
  47.7 12.3 %copy-start.2 = (bf16[256,384]{1,0:T(8,128)(2,1)S(1)}, bf16[256,384]{1,0:T(8,128)(2,1)}, u32[]{:S(2)}) copy-start(bf16[256,384]{1,0:T(8,128)(2,1)} %copy-done.1) | copy-start | bytes 589828
  47.7 12.3 %copy-start.6 = (bf16[1,2,4,32,384]{4,3,2,1,0:T(8,128)(2,1)S(1)}, bf16[1,2,4,32,384]{4,3,2,1,0:T(8,128)(2,1)}, u32[]{:S(2)}) copy-start(bf16[1,2,4,32,384]{4,3,2,1,0:T(8,128)(2,1)} %get-tuple-element.15) | copy-start | bytes 589828
  56.5 3.8 %copy-start = (f32[4,128,384]{2,1,0:T(8,128)}, f32[4,128,384]{2,1,0:T(8,128)S(1)}, u32[]{:S(2)}) copy-start(f32[4,128,384]{2,1,0:T(8,128)S(1)} %conv_data_grad.1) | copy-start | bytes 2359300
  57.2 95.0 %collective-permute-start = (bf16[2,4,32,384]{3,2,1,0:T(8,128)(2,1)}, bf16[2,4,32,384]{3,2,1,0:T(8,128)(2,1)}, u32[]{:S(2)}, u32[]{:S(2)}) collective-permute-start(bf16[2,4,32,384]{3,2,1,0:T(8,128)(2,1)} %bitcast.25), channel_id=1, source_target_pairs={{8,0},{16,8},{24,16},{9,1},{17,9},{25,17},{10,2},{18,10},{26,18},{... | collective-permute-start | bytes 589832 | tf_op jit(solution)/shard_map/ppermute | solution.py:17
  148.0 4.2 %slice-start = ((f32[4,128,384]{2,1,0:T(8,128)}), f32[2,128,384]{2,1,0:T(8,128)S(1)}, s32[]{:S(2)}) async-start(f32[4,128,384]{2,1,0:T(8,128)} %copy-done), calls=%async_computation | async-start | bytes 786432 | tf_op jit(solution)/shard_map/slice | solution.py:439
